TPU v7x, 32 devices: a whole 2x2x4 slice. The times are simulated.
32 devices in a mesh: freq: 2 (over y), tm: 16 (over z, x, core).
Axes of the slice: x: 2, y: 2, z: 4, core: 2. Of those that a mesh axis runs over, the one named last changes fastest.
Arguments:
- audio: bfloat16 [16, 2097152], P('tm', 'freq'), may hold values from -8 to 8
- w_start: float32 [32, 4096], P(None, 'freq'), may hold values from 0.05 to 0.5
- h_start: float32 [32, 4096], P(None, 'tm'), may hold values from 0.05 to 0.5
Outputs:
- components: float32 [32, 4096], P(None, 'freq')
- activations: float32 [32, 4096], P(None, 'tm')
All inputs are finite; a program needn't handle non-finite values.
Results may differ from a plain program's by a relative error of at most 0.00053.
Values may be sent and summed in bfloat16 or wider, within the bound.
No kernel may reach another device: no remote copies, remote signals or barrier semaphores. Data moves between devices by JAX's collectives and lax.ppermute only.
A program may use at most 64 MiB of HBM per device.

v0:
```python
import functools
import math

import jax
import jax.numpy as jnp
import numpy as np
from jax import lax
from jax.experimental import pallas as pl
from jax.experimental.pallas import tpu as pltpu
from jax.sharding import PartitionSpec as P

ITERS = 2
HIGHEST = lax.Precision.HIGHEST
ALL = ("freq", "tm")
LANES = 128
OUTER = 64
HALF = OUTER // 2
FRAME = OUTER * LANES
CHUNK = 16
PAIR = 2
GROUP = 4
NT = (((1,), (1,)), ((), ()))
LEAST = 2.0**-126


def tables():
    a = np.arange(OUTER)
    i = np.arange(LANES)
    r = np.arange(HALF)
    position = a[:, None] * LANES + i[None, :]
    window = 0.5 - 0.5 * np.cos(2 * np.pi * position / FRAME)
    window = window / math.sqrt(0.375 * FRAME)
    angle = 2 * np.pi * (r[:, None] * a[None, :] % OUTER) / OUTER
    first = np.stack([np.cos(angle), -np.sin(angle)], axis=1).reshape(2 * HALF, OUTER)
    first[1] = np.cos(np.pi * a)
    turn = 2 * np.pi * r[:, None] * i[None, :] / FRAME
    turn_cos = np.cos(turn)
    turn_sin = np.sin(turn)
    m = np.arange(OUTER)
    column = np.concatenate([m, LANES - 1 - m])
    angle = 2 * np.pi * (i[:, None] * column[None, :] % LANES) / LANES
    top = np.concatenate([np.cos(angle), -np.sin(angle)], axis=1)
    bottom = np.concatenate([np.sin(angle), np.cos(angle)], axis=1)
    second = np.concatenate([top, bottom], axis=0)
    zero = np.zeros((LANES, OUTER))
    angle_a = 2 * np.pi * i[:, None] * (m * OUTER)[None, :] / FRAME
    angle_b = 2 * np.pi * i[:, None] * (m * OUTER + HALF)[None, :] / FRAME
    top = np.concatenate([np.cos(angle_a), zero, -np.sin(angle_a), zero], axis=1)
    bottom = np.concatenate([zero, np.cos(angle_b), zero, -np.sin(angle_b)], axis=1)
    edge = np.concatenate([top, bottom], axis=0)

    first = np.concatenate([first, np.zeros((OUTER, LANES - OUTER))], axis=1)
    second, edge = (np.concatenate([t[:, :LANES], t[:, LANES:]], axis=0) for t in (second, edge))
    parts = [window, first, turn_cos, turn_sin, second, edge]
    return np.concatenate(parts, axis=0).astype(np.float32)


def halves(value):
    high = value.astype(jnp.bfloat16)
    return high, (value - high.astype(jnp.float32)).astype(jnp.bfloat16)


def spectrum_kernel(core, audio, source, keep, give, peak, heard, table, stack, held, audio_sems, table_sems):
    frames = keep.shape[1]
    chunks = frames // CHUNK
    turns = 2 * OUTER

    def audio_copy(chunk):
        span = pl.ds(pl.multiple_of(chunk * CHUNK * FRAME, CHUNK * FRAME), CHUNK * FRAME)
        return pltpu.make_async_copy(audio.at[:, span], heard.at[chunk], audio_sems.at[chunk])

    def table_copy(k):
        span = pl.ds(0, turns) if k == 0 else pl.ds(turns, table.shape[0] - turns)
        return pltpu.make_async_copy(source.at[span], table.at[span], table_sems.at[k])

    table_copy(0).start()
    for chunk in range(chunks):
        audio_copy(chunk).start()
    table_copy(1).start()
    table_copy(0).wait()
    high, low = halves(table[OUTER:turns, :OUTER])
    first_terms = jnp.concatenate([high, low, high], axis=1)

    @pl.loop(0, chunks)
    def _(chunk):
        audio_copy(chunk).wait()
        samples = heard[chunk].reshape(CHUNK * OUTER, LANES).astype(jnp.float32)
        shape = table[:OUTER]
        for start in range(0, CHUNK, PAIR):
            columns = []
            for frame in range(start, start + PAIR):
                high, low = halves(samples[frame * OUTER : (frame + 1) * OUTER] * shape)
                columns.append(jnp.concatenate([high, high, low], axis=0))
            sums = jnp.dot(
                first_terms, jnp.concatenate(columns, axis=1), preferred_element_type=jnp.float32
            )
            for frame in range(start, start + PAIR):
                place = pl.ds(chunk * CHUNK + frame, OUTER, stride=frames + 1)
                held[place, :] = sums[:, (frame - start) * LANES : (frame - start + 1) * LANES]

    table_copy(1).wait()
    for k in range(2):
        at = turns + 2 * HALF + k * 4 * LANES
        both = jnp.concatenate([table[at : at + 2 * LANES], table[at + 2 * LANES : at + 4 * LANES]], axis=1)
        high, low = halves(both)
        stack[k] = jnp.concatenate([high, low, high], axis=0)

    def turned(row):
        at = row * 2 * (frames + 1)
        real = held[pl.ds(at, frames), :]
        imag = held[pl.ds(at + frames + 1, frames), :]
        cos, sin = table[pl.ds(turns + row, 1), :], table[pl.ds(turns + HALF + row, 1), :]
        high_r, low_r = halves(real * cos + imag * sin)
        high_i, low_i = halves(imag * cos - real * sin)
        return jnp.concatenate([high_r, high_i, high_r, high_i, low_r, low_i], axis=1)

    def magnitude(terms, k):
        bins = jnp.dot(terms, stack[k], preferred_element_type=jnp.float32)
        real, imag = bins[:, :LANES], bins[:, LANES:]
        square = real * real + imag * imag
        found = (square * lax.rsqrt(jnp.maximum(square, LEAST))).astype(keep.dtype)
        peak[...] = jnp.maximum(peak[...], jnp.max(found.reshape(-1, 16, LANES), axis=0))
        return found

    peak[...] = jnp.zeros_like(peak)

    def rows_of(side, out):
        for group in range(HALF // 2 // GROUP):
            start = side * (HALF // 2) + group * GROUP
            found = magnitude(jnp.concatenate([turned(start + k) for k in range(GROUP)], axis=0), 0)
            for k in range(GROUP):
                out[group * GROUP + k] = found[k * frames : (k + 1) * frames]

    rows_of(1 - core[0], give)
    rows_of(core[0], keep)
    edge = magnitude(turned(0), 1)

    @pl.when(core[0] == 0)
    def _():
        keep[0] = edge

    @pl.when(core[0] != 0)
    def _():
        give[0] = edge


def spectrum(audio, core):
    frames = audio.shape[1] // FRAME
    table = jnp.asarray(tables())
    far = pl.BlockSpec(memory_space=pltpu.HBM)
    return pl.pallas_call(
        spectrum_kernel,
        out_shape=[jax.ShapeDtypeStruct((HALF // 2, frames, LANES), jnp.bfloat16)] * 2
        + [jax.ShapeDtypeStruct((16, LANES), jnp.bfloat16)],
        in_specs=[pl.BlockSpec(memory_space=pltpu.SMEM), far, far],
        out_specs=[pl.BlockSpec(memory_space=pltpu.VMEM)] * 3,
        scratch_shapes=[
            pltpu.VMEM((frames // CHUNK, 1, CHUNK * FRAME), jnp.bfloat16),
            pltpu.VMEM(table.shape, table.dtype),
            pltpu.VMEM((2, 6 * LANES, 2 * LANES), jnp.bfloat16),
            pltpu.VMEM((OUTER * (frames + 1), LANES), jnp.float32),
            pltpu.SemaphoreType.DMA((frames // CHUNK,)),
            pltpu.SemaphoreType.DMA((2,)),
        ],
        compiler_params=pltpu.CompilerParams(vmem_limit_bytes=105 * 2**19),
        cost_estimate=pl.CostEstimate(
            flops=6 * frames * FRAME * (OUTER + 2 * LANES), bytes_accessed=2**22, transcendentals=0
        ),
        name="spectrum",
    )(core, audio, table)


def update(state, numer, gram):
    return state * numer / jnp.dot(gram, state, precision=HIGHEST, preferred_element_type=jnp.float32)


def step_kernel(comps, grid, acts, parts, acts_out):
    rows, comp, lanes = comps.shape
    wide = jnp.concatenate([comps[r] for r in range(rows)], axis=1)
    tall = jnp.concatenate([grid[r] for r in range(rows)], axis=1)
    numer = lax.dot_general(wide.astype(jnp.bfloat16), tall, NT, preferred_element_type=jnp.float32)
    gram = lax.dot_general(wide, wide, NT, precision=HIGHEST, preferred_element_type=jnp.float32)
    acts_new = update(acts[...], numer, gram)
    acts_out[...] = acts_new
    gram = lax.dot_general(acts_new, acts_new, NT, precision=HIGHEST, preferred_element_type=jnp.float32)
    per = LANES // comp
    high = comp // per
    packed = jnp.concatenate([gram[j * high : (j + 1) * high] for j in range(per)], axis=1)
    sums = jnp.dot(acts_new.astype(jnp.bfloat16), tall, preferred_element_type=jnp.float32)
    for r in range(rows):
        parts[r, :comp, :] = sums[:, r * lanes : (r + 1) * lanes]
        parts[r, comp:, :] = packed


def advance(comps, grid, acts):
    rows, comp, lanes = comps.shape
    extra = comp * comp // LANES
    return pl.pallas_call(
        step_kernel,
        out_shape=(
            jax.ShapeDtypeStruct((rows, comp + extra, lanes), jnp.float32),
            jax.ShapeDtypeStruct(acts.shape, jnp.float32),
        ),
        compiler_params=pltpu.CompilerParams(vmem_limit_bytes=32 * 2**20),
        name="advance",
    )(comps, grid, acts)


def unpack(packed):
    high = packed.shape[0]
    comp = math.isqrt(packed.size)
    return packed.reshape(high, LANES // comp, comp).transpose(1, 0, 2).reshape(comp, comp)


def inner_order(natural):
    comp = natural.shape[0]
    cube = natural.reshape(comp, -1, OUTER).transpose(2, 0, 1)
    mirrored = jnp.concatenate([cube[HALF : HALF + 1], cube[: HALF : -1]], axis=0)
    return jnp.concatenate([cube[:HALF], mirrored], axis=2)


def natural_order(inner):
    comp, width = inner.shape[1], inner.shape[2] // 2
    low, mirrored = inner[:, :, :width], inner[:, :, width:]
    cube = jnp.concatenate([low, mirrored[:1], mirrored[:0:-1]], axis=0)
    return cube.transpose(1, 2, 0).reshape(comp, -1)


def gather_freq(block, n_freq, at):
    pieces = [block]
    for shift in range(1, n_freq):
        ring = [(i, (i + shift) % n_freq) for i in range(n_freq)]
        pieces.append(lax.ppermute(block, "freq", ring))
    placed = []
    for p in range(n_freq):
        value = pieces[0]
        for shift in range(1, n_freq):
            value = jnp.where((at - shift) % n_freq == p, pieces[shift], value)
        placed.append(value)
    return jnp.concatenate(placed, axis=1)


TOP = 13
SIDE = HALF // 2


def pack(gram):
    comp = gram.shape[0]
    per = LANES // comp
    high = comp // per
    return jnp.concatenate([gram[j * high : (j + 1) * high] for j in range(per)], axis=1)


def unpacked(packed):
    comp = math.isqrt(packed.size)
    return jnp.concatenate([packed[:, j * comp : (j + 1) * comp] for j in range(LANES // comp)], axis=0)


def exponent(value):
    peak = jnp.max(jnp.abs(value), axis=(0, 1), keepdims=True)
    return jnp.floor(jnp.log2(jnp.maximum(peak, 1e-30))) - TOP


def power(exps):
    count = jnp.abs(exps).astype(jnp.int32)
    value = jnp.ones_like(exps)
    for bit in range(7):
        step = jnp.where(exps < 0, 2.0 ** -(2**bit), 2.0 ** (2**bit))
        value = value * jnp.where((count >> bit) & 1 == 1, step, 1.0)
    return value


def places(shape):
    return [lax.broadcasted_iota(jnp.int32, shape, axis) for axis in range(2)]


def mirrored_at(r):
    return OUTER - r if r else HALF


def gram_of(value):
    rows = value.shape[0]
    both = jnp.concatenate(halves(value), axis=0)
    parts = lax.dot_general(both, both, NT, preferred_element_type=jnp.float32)
    cross = parts[:rows, rows:] + parts[rows:, :rows]
    return parts[:rows, :rows] + (cross + parts[rows:, rows:])


def start_kernel(at, own, other, keep, give, acts, acts_out, mine, held):
    comp = own.shape[0]
    row, side, first = at[0], at[1], at[2] == 0
    wide = jnp.concatenate(
        [jnp.where(first, own[...], other[...]), jnp.where(first, other[...], own[...])], axis=1
    )
    quads, eighth = LANES // comp, 8
    for q in range(eighth):
        columns = [wide[:, (c * eighth + q) * LANES : (c * eighth + q + 1) * LANES] for c in range(quads)]
        turned = jnp.concatenate(columns, axis=0).T
        for m in range(2):
            place = (2 * q + m) * (OUTER + 1)
            held[place : place + OUTER, :] = turned[m * OUTER : (m + 1) * OUTER]
    gram = gram_of(wide)
    span = OUTER // quads
    block = places((span, LANES))[1] // comp

    def pair(r):
        mirror = jnp.where(r == 0, HALF, OUTER - r)
        return [held[pl.ds(j, span, stride=OUTER + 1), :] for j in (r, mirror)]

    both = jnp.concatenate(pair(row), axis=0).T
    mine[...] = jnp.concatenate(
        [
            both[c * comp : (c + 1) * comp, h * span : (h + 1) * span]
            for h in range(2)
            for c in range(quads)
        ],
        axis=1,
    )
    total = jnp.zeros((acts.shape[1], LANES), jnp.float32)
    batch = 8
    for grid, start in ((keep, side * SIDE), (give, (1 - side) * SIDE)):
        for base in range(0, SIDE, batch):
            pieces = []
            for u in range(base, base + batch):
                for value in pair(start + u):
                    pieces += [jnp.where(block == c, value, 0.0).astype(jnp.bfloat16) for c in range(quads)]
            left = jnp.concatenate([grid[u] for u in range(base, base + batch)], axis=1)
            total += jnp.dot(left, jnp.concatenate(pieces, axis=0), preferred_element_type=jnp.float32)
    total = total.T
    numer = sum(total[c * comp : (c + 1) * comp] for c in range(quads))
    acts_out[...] = update(acts[...], numer, gram)


def sealed(sums, gram, squares, bound=None):
    comp = gram.shape[0]
    sums_exp, gram_exp = exponent(sums if bound is None else bound), exponent(squares)
    packed = pack(gram) * power(-gram_exp)
    rows, lanes = places(packed.shape)
    last, end = packed.shape[0] - 1, LANES - comp
    packed = jnp.where((rows == last) & (lanes == end), sums_exp, packed)
    packed = jnp.where((rows == last) & (lanes == end + 1), gram_exp, packed)
    return sums * power(-sums_exp), packed


def opened(got, comp):
    end = LANES - comp
    scales = power(got[:, got.shape[1] - 1, :])
    sources = range(got.shape[0])
    gram = sum(got[s, comp:, :] * scales[s : s + 1, end + 1 : end + 2] for s in sources)
    gram = unpacked(gram)
    at = places(gram.shape)
    for column in range(2):
        mirrored = gram[column : column + 1, comp - 1 : comp]
        gram = jnp.where((at[0] == comp - 1) & (at[1] == column), mirrored, gram)
    return [scales[s : s + 1, end : end + 1] for s in sources], gram


def tall(grid):
    return jnp.concatenate([grid[u] for u in range(SIDE)], axis=1)


def finish(acts, grids, parts, peak=None):
    comp = acts[0].shape[0]
    sums, gram, weight, squares = 0.0, 0.0, 0.0, 0.0
    for value, grid in zip(acts, grids):
        left = value.astype(jnp.bfloat16)
        weight += jnp.sum(left.astype(jnp.float32), axis=1, keepdims=True)
        squares += jnp.sum(value * value, axis=1, keepdims=True)
        sums += jnp.dot(left, tall(grid), preferred_element_type=jnp.float32)
        gram += lax.dot_general(value, value, NT, precision=HIGHEST, preferred_element_type=jnp.float32)
    sums, packed = sealed(sums, gram, squares, None if peak is None else weight * (1.01 * peak))
    for u in range(SIDE):
        parts[u, :comp, :] = sums[:, u * LANES : (u + 1) * LANES]
        parts[u, comp:, :] = packed


def sums_kernel(acts, sibling, keep, taken, parts):
    finish((acts[...], sibling[...]), (keep, taken), parts)


def partial_kernel(got, keep, taken, peak, out):
    comp = out.shape[0] - got.shape[1]
    scales, gram = opened(got, comp)
    wide = [(got[u, :comp, :] * scales[u]).astype(jnp.bfloat16) for u in range(SIDE)]
    wide = jnp.concatenate(wide, axis=1)
    for k, grid in enumerate((keep, taken)):
        out[k * comp : (k + 1) * comp, :] = lax.dot_general(
            wide, tall(grid), NT, preferred_element_type=jnp.float32
        )
    packed = pack(gram)
    rows, lanes = places(packed.shape)
    highest = jnp.max(peak[...].astype(jnp.float32), axis=(0, 1), keepdims=True)
    place = (rows == packed.shape[0] - 1) & (lanes == LANES - comp)
    out[2 * comp :, :] = jnp.where(place, highest, packed)


def again_kernel(half, other_half, acts, sibling, keep, taken, parts, acts_out):
    comp = acts.shape[0]
    mine, theirs = half[2 * comp :, :], other_half[2 * comp :, :]
    last, end = mine.shape[0] - 1, LANES - comp
    peak = jnp.maximum(mine, theirs)[last : last + 1, end : end + 1]
    gram = unpacked(mine + theirs)
    at = places(gram.shape)
    gram = jnp.where((at[0] == comp - 1) & (at[1] == 0), gram[:1, comp - 1 : comp], gram)
    new = update(acts[...], half[:comp, :] + other_half[comp : 2 * comp, :], gram)
    sibling_new = update(sibling[...], half[comp : 2 * comp, :] + other_half[:comp, :], gram)
    acts_out[...] = new
    finish((new, sibling_new), (keep, taken), parts, peak)


def slice_kernel(got, mine, out, payload):
    comp = mine.shape[0]
    scales, gram = opened(got, comp)
    sums = sum(got[s, :comp, :] * scales[s] for s in range(got.shape[0]))
    new = update(mine[...], sums, gram)
    out[...] = new
    gram = lax.dot_general(new, new, NT, precision=HIGHEST, preferred_element_type=jnp.float32)
    squares = jnp.sum(new * new, axis=1, keepdims=True)
    sums, packed = sealed(new.astype(jnp.bfloat16).astype(jnp.float32), gram, squares)
    payload[:comp, :] = sums
    payload[comp:, :] = packed


def last_kernel(got, mine, out, exps_out):
    comp = mine.shape[0]
    scales, gram = opened(got, comp)
    sums = sum(got[s, :comp, :] * scales[s] for s in range(got.shape[0]))
    new = update(mine[...], sums, gram)
    at = places(gram.shape)
    diagonal = jnp.sum(jnp.where(at[0] == at[1], gram, 0.0), axis=1, keepdims=True)
    bound = sum(scales) * 2.0 ** (TOP + 1) / jnp.maximum(diagonal, 1e-30)
    exps = jnp.clip(jnp.floor(jnp.log2(jnp.maximum(bound, 1e-30))), -100, 100) - TOP
    exps_out[...] = jnp.broadcast_to(exps, exps_out.shape)
    turned = (new * power(-exps)).T
    span = OUTER // 4
    for freq in range(2):
        starts = [h * OUTER + freq * 2 * span + half * span for h in range(2) for half in range(2)]
        out[freq] = jnp.concatenate([turned[a : a + span] for a in starts], axis=1)


def natural_kernel(at, got, exps, acts, partner, out, acts_out, low, high):
    comp = out.shape[0]
    span = OUTER // 4
    for r in range(HALF):
        value = got[r % SIDE * 2 + r // SIDE]
        low[pl.ds(r, span, stride=HALF + 1), :] = value
        high[pl.ds(mirrored_at(r) % HALF, span, stride=HALF + 1), :] = pltpu.roll(value, LANES // 2, 1)
    factor = power(exps[...])
    for pair in range(span // 2):
        rows = []
        for place in (2 * pair, 2 * pair + 1):
            begin = place * (HALF + 1)
            rows += [ref[begin : begin + HALF, :] for ref in (low, high)]
        turned = jnp.concatenate(rows, axis=0).T
        for half in range(2):
            begin = (half * (span // 2) + pair) * LANES
            out[:, begin : begin + LANES] = turned[half * comp : (half + 1) * comp] * factor
    first, own, other = at[2] == 0, acts[...], partner[...]
    acts_out[...] = jnp.concatenate([jnp.where(first, own, other), jnp.where(first, other, own)], axis=1)


def local(kernel, outs, name, *arrays, scratch=(), cost=None):
    vmem = pl.BlockSpec(memory_space=pltpu.VMEM)
    smem = pl.BlockSpec(memory_space=pltpu.SMEM)
    many = isinstance(outs, list)
    shapes = [jax.ShapeDtypeStruct(shape, dtype) for shape, dtype in (outs if many else [outs])]
    return pl.pallas_call(
        kernel,
        out_shape=shapes if many else shapes[0],
        in_specs=[smem if a.dtype == jnp.int32 else vmem for a in arrays],
        out_specs=[vmem] * len(outs) if many else vmem,
        scratch_shapes=list(scratch),
        compiler_params=pltpu.CompilerParams(vmem_limit_bytes=32 * 2**20),
        cost_estimate=cost,
        name=name,
    )(*arrays)


def row_shards(audio, w_start, h_start):
    f16, f32 = jnp.float16, jnp.float32
    comp = w_start.shape[0]
    swap = [(0, 1), (1, 0)]
    freq_at, core_at = lax.axis_index("freq"), lax.axis_index("core")
    q = freq_at * lax.axis_size("chips") + lax.axis_index("chips")
    at = jnp.stack([core_at * SIDE + q, core_at, freq_at]).astype(jnp.int32)
    other = lax.ppermute(w_start, "freq", swap)
    keep, give, peak = spectrum(audio, at[1:2])
    frames = keep.shape[1]
    extra = comp * comp // LANES
    taken = lax.ppermute(give, "core", swap)
    acts = lax.dynamic_slice_in_dim(h_start, freq_at * frames, frames, 1)
    message = ((SIDE, comp + extra, LANES), f32)
    lane_rows = ((comp, LANES), f32)

    def exchange(value, axes=("freq", "chips")):
        value = lax.all_to_all(value.astype(f16), axes, split_axis=0, concat_axis=0, tiled=True)
        return value.astype(f32)

    acts, mine = local(
        start_kernel,
        [(acts.shape, f32), lane_rows],
        "start",
        at,
        w_start,
        other,
        keep,
        give,
        acts,
        scratch=[pltpu.VMEM((LANES // 8 * (OUTER + 1), LANES), f32)],
        cost=pl.CostEstimate(flops=2**34, bytes_accessed=2**25, transcendentals=0),
    )
    sibling = lax.ppermute(acts, "core", swap)
    parts = local(sums_kernel, message, "sums", acts, sibling, keep, taken)
    for step in range(ITERS - 1):
        got = exchange(parts)
        outs = [lane_rows, ((comp + extra, LANES), f32)]
        mine, payload = local(slice_kernel, outs, "slice", got, mine)
        got = exchange(jnp.broadcast_to(payload, (SIDE,) + payload.shape))
        half = local(partial_kernel, ((2 * comp + extra, LANES), f32), "partial", got, keep, taken, peak)
        other_half = lax.ppermute(half, "core", swap)
        outs = [message, (acts.shape, f32)]
        parts, acts = local(
            again_kernel, outs, "again", half, other_half, acts, sibling, keep, taken
        )
    got = exchange(parts)
    acts, got = lax.optimization_barrier((acts, got))
    partner = lax.ppermute(acts, "freq", swap)
    final, exps = local(last_kernel, [((2, OUTER // 4, LANES), f32), lane_rows], "last", got, mine)
    final = jnp.broadcast_to(final[:, None], (2, HALF // 2) + final.shape[1:])
    got = exchange(final.reshape((HALF,) + final.shape[2:]), ("freq", "chips", "core"))
    return local(
        natural_kernel,
        [(w_start.shape, f32), (h_start.shape, f32)],
        "natural",
        at,
        got,
        exps,
        acts,
        partner,
        scratch=[pltpu.VMEM((OUTER // 4 * (HALF + 1), LANES), f32)] * 2,
    )


def shards(n_freq, n_tm, audio, w_start, h_start):
    n_dev = n_freq * n_tm
    comp, w_cols = w_start.shape
    bins = w_cols * n_freq
    own = bins // n_dev
    width = OUTER // n_freq
    freq_at = lax.axis_index("freq")
    me = freq_at * n_tm + lax.axis_index("tm")
    grid = jnp.concatenate(spectrum(audio, jnp.zeros((1,), jnp.int32))[:2], axis=0)
    frames = grid.shape[1]
    comps = inner_order(gather_freq(w_start, n_freq, freq_at))
    acts = lax.dynamic_slice_in_dim(h_start, freq_at * frames, frames, 1)
    per_row = LANES // own
    mine = lax.dynamic_slice(
        comps, (me // per_row, 0, me % per_row * own), (1, comp, own)
    ).reshape(comp, own)
    for step in range(ITERS):
        parts, acts = advance(comps, grid, acts)
        sums = parts[:, :comp].reshape(HALF, comp, per_row, own).transpose(0, 2, 1, 3)
        gram = jnp.broadcast_to(parts[0, comp:].reshape(1, -1), (n_dev, comp * comp))
        parts = jnp.concatenate([sums.reshape(n_dev, -1), gram], axis=1).reshape(n_dev, -1, LANES)
        got = lax.all_to_all(parts, ALL, split_axis=0, concat_axis=0, tiled=True)
        value = jnp.sum(got, axis=0)
        rows = comp * own // LANES
        mine = update(mine, value[:rows].reshape(comp, own), unpack(value[rows:]))
        every = jnp.broadcast_to(mine.reshape(1, -1, LANES), (n_dev, rows, LANES))
        comps = lax.all_to_all(every, ALL, split_axis=0, concat_axis=0, tiled=True)
        comps = comps.reshape(HALF, per_row, comp, own).transpose(0, 2, 1, 3)
        comps = comps.reshape(HALF, comp, LANES)
    cut = lax.dynamic_slice_in_dim(comps.reshape(HALF, comp, 2, OUTER), freq_at * width, width, 3)
    components = natural_order(cut.reshape(HALF, comp, 2 * width))
    activations = gather_freq(acts, n_freq, freq_at)
    return (components, activations)


def solution(mesh):
    sizes = (mesh.shape["freq"], mesh.shape["tm"])
    if sizes == (2, SIDE):
        devices = mesh.devices.reshape(2, SIDE // 2, 2)
        mesh = jax.sharding.Mesh(devices, ("freq", "chips", "core"))
        body, tm = row_shards, ("chips", "core")
    else:
        body, tm = functools.partial(shards, *sizes), "tm"
    return jax.shard_map(
        body,
        mesh=mesh,
        in_specs=(P(tm, "freq"), P(None, "freq"), P(None, tm)),
        out_specs=(P(None, "freq"), P(None, tm)),
        check_vma=False,
    )
```

profile of v0, /device:TPU:0, one launch (start us, length us, event | category | flops | bytes accessed | tf_op | source)
XLA Modules:
  0.0 67.9 jit_solution(12416217852284709864)
XLA Ops:
  0.6 0.0 copy-start
  0.6 0.0 copy-start.1
  0.7 3.0 %collective-permute-start = (f32[32,2048]{1,0:T(8,128)}, f32[32,2048]{1,0:T(8,128)S(1)}, u32[]{:S(2)}, u32[]{:S(2)}) collective-permute-start(f32[32,2048]{1,0:T(8,128)} %own.1), channel_id=1, source_target_pairs={{0,16},{16,0},{1,17},{17,1},{2,18},{18,2},{3,19},{19,3},{4,20},{20... | collective-permute-start | bytes 786440 | tf_op jit(solution)/shard_map/ppermute | solution.py:486
  3.7 6.1 %spectrum.1 = (bf16[16,128,128]{2,1,0:T(8,128)(2,1)S(1)}, bf16[16,128,128]{2,1,0:T(8,128)(2,1)S(1)}, bf16[16,128]{1,0:T(8,128)(2,1)S(1)}) custom-call(s32[1]{0:T(128)} %bitcast.1.core, bf16[1,1048576]{1,0:T(2,128)(2,1)} %audio.1, f32[1216,128]{1,0:T(8,128)} %constant.24.clone.source), custom_call_target="tpu_custom_call" | custom-call | flops 2013265920 | bytes 4194304 | tf_op jit(solution)/shard_map/spectrum/pallas_call | solution.py:151
  9.8 0.1 collective-permute-start.2
  9.9 0.1 pad_add_fusion.at
  10.0 0.0 copy-done
  10.0 0.2 collective-permute-done.other
  10.2 0.0 copy-done.1
  10.2 1.4 %start.1 = (f32[32,128]{1,0:T(8,128)S(1)}, f32[32,128]{1,0:T(8,128)S(1)}) custom-call(s32[3]{0:T(128)S(1)} %pad_add_fusion.at, f32[32,2048]{1,0:T(8,128)S(1)} %copy-done.1, f32[32,2048]{1,0:T(8,128)S(1)} %collective-permute-done.other, bf16[16,128,128]{2,1,0:T(8,128)(2,1)S(1)} %get-tuple-element.15.keep, bf16[16,128,128]{2,1,0:T(8,128)(2,1)S(1)} %get-tuple-element.16.give, ...), custom_call_target="tpu_custom_call" | custom-call | flops 17179869184 | bytes 33554432 | tf_op jit(solution)/shard_map/start/pallas_call | solution.py:467
  11.6 0.4 collective-permute-start.1
  12.0 0.9 %collective-permute-done.1.sibling = f32[32,128]{1,0:T(8,128)S(1)} collective-permute-done((f32[32,128]{1,0:T(8,128)S(1)}, f32[32,128]{1,0:T(8,128)S(1)}, u32[]{:S(2)}, u32[]{:S(2)}) %collective-permute-start.1) | collective-permute-done | bytes 16416 | tf_op jit(solution)/shard_map/ppermute | solution.py:512
  12.8 0.0 collective-permute-done.2.taken
  12.9 0.5 sums.1
  13.4 15.0 %all_to_all.20 = f16[16,40,128]{2,1,0:T(8,128)(2,1)S(1)} all-to-all(f16[16,40,128]{2,1,0:T(8,128)(2,1)S(1)} %convert_element_type.29), channel_id=1, replica_groups=mesh['freq'=2,'chips'=8,'core'=2] {'freq','chips'}, dimensions={0} | all-to-all | bytes 327680 | tf_op jit(solution)/shard_map/all_to_all | solution.py:496
  28.5 0.7 %slice.1 = (f32[32,128]{1,0:T(8,128)S(1)}, f32[40,128]{1,0:T(8,128)S(1)}) custom-call(f32[16,40,128]{2,1,0:T(8,128)S(1)} %convert_element_type.30.got, f32[32,128]{1,0:T(8,128)S(1)} %get-tuple-element.18.mine), custom_call_target="tpu_custom_call" | custom-call | tf_op jit(solution)/shard_map/slice/pallas_call | solution.py:467
  29.2 11.1 %all_to_all.21 = f16[16,40,128]{2,1,0:T(8,128)(2,1)S(1)} all-to-all(f16[16,40,128]{2,1,0:T(8,128)(2,1)S(1)} %broadcast_in_dim.4), channel_id=1, replica_groups=mesh['freq'=2,'chips'=8,'core'=2] {'freq','chips'}, dimensions={0} | all-to-all | bytes 327680 | tf_op jit(solution)/shard_map/all_to_all | solution.py:496
  40.4 0.7 %partial.1.half = f32[72,128]{1,0:T(8,128)S(1)} custom-call(f32[16,40,128]{2,1,0:T(8,128)S(1)} %convert_element_type.32.got, bf16[16,128,128]{2,1,0:T(8,128)(2,1)S(1)} %get-tuple-element.15.keep, bf16[16,128,128]{2,1,0:T(8,128)(2,1)S(1)} %collective-permute-done.2.taken, bf16[16,128]{1,0:T(8,128)(2,1)S(1)} %get-tuple-element.20.peak), custom_call_target="tpu_custom_call" | custom-call | tf_op jit(solution)/shard_map/partial/pallas_call | solution.py:467
  41.1 0.0 collective-permute-start.3
  41.1 1.2 %collective-permute-done.3.other_half = f32[72,128]{1,0:T(8,128)S(1)} collective-permute-done((f32[72,128]{1,0:T(8,128)S(1)}, f32[72,128]{1,0:T(8,128)S(1)}, u32[]{:S(2)}, u32[]{:S(2)}) %collective-permute-start.3) | collective-permute-done | bytes 36896 | tf_op jit(solution)/shard_map/ppermute | solution.py:520
  42.3 0.7 again.1
  43.0 11.0 %all_to_all.22 = f16[16,40,128]{2,1,0:T(8,128)(2,1)S(1)} all-to-all(f16[16,40,128]{2,1,0:T(8,128)(2,1)S(1)} %convert_element_type.33), channel_id=1, replica_groups=mesh['freq'=2,'chips'=8,'core'=2] {'freq','chips'}, dimensions={0} | all-to-all | bytes 327680 | tf_op jit(solution)/shard_map/all_to_all | solution.py:496
  54.1 0.7 last.1
  54.8 0.7 broadcast_in_dim.10
  55.4 2.6 %all-to-all-start.3 = ((f16[32,16,128]{2,1,0:T(8,128)(2,1)}), f16[32,16,128]{2,1,0:T(8,128)(2,1)S(1)}, u32[]{:S(2)}, u32[]{:S(2)}) async-start(f16[32,16,128]{2,1,0:T(8,128)(2,1)} %bitcast.3), calls=%async_computation.3 | async-start | bytes 262144 | tf_op jit(solution)/shard_map/all_to_all | solution.py:496
  58.0 1.7 %collective-permute-start.4 = (f32[32,128]{1,0:T(8,128)S(1)}, f32[32,128]{1,0:T(8,128)S(1)}, u32[]{:S(2)}, u32[]{:S(2)}) collective-permute-start(f32[32,128]{1,0:T(8,128)S(1)} %get-tuple-element.27.acts), channel_id=1, source_target_pairs={{0,16},{16,0},{1,17},{17,1},{2,18},{18,2},{3,19},{19,3},{4,20},{20... | collective-permute-start | bytes 49160 | tf_op jit(solution)/shard_map/ppermute | solution.py:527
  59.7 6.5 %all-to-all-done.3 = f16[32,16,128]{2,1,0:T(8,128)(2,1)S(1)} async-done(((f16[32,16,128]{2,1,0:T(8,128)(2,1)}), f16[32,16,128]{2,1,0:T(8,128)(2,1)S(1)}, u32[]{:S(2)}, u32[]{:S(2)}) %all-to-all-start.3) | async-done | bytes 131104 | tf_op jit(solution)/shard_map/all_to_all | solution.py:496
  66.3 0.0 collective-permute-done.4.partner
  66.3 1.6 %natural.1 = (f32[32,2048]{1,0:T(8,128)}, f32[32,256]{1,0:T(8,128)}) custom-call(s32[3]{0:T(128)S(1)} %pad_add_fusion.at, f32[32,16,128]{2,1,0:T(8,128)S(1)} %convert_element_type.37.got, f32[32,128]{1,0:T(8,128)S(1)} %get-tuple-element.26.exps, f32[32,128]{1,0:T(8,128)S(1)} %get-tuple-element.27.acts, f32[32,128]{1,0:T(8,128)S(1)} %collective-permute-done.4.partner), custom_call_target="tpu_custom_call" | custom-call | tf_op jit(solution)/shard_map/natural/pallas_call | solution.py:467
  (10 shorter events, 0.2 us)
Async XLA Ops:
  0.6 9.4 %copy-start = (f32[32,256]{1,0:T(8,128)S(1)}, f32[32,256]{1,0:T(8,128)}, u32[]{:S(2)}) copy-start(f32[32,256]{1,0:T(8,128)} %param.6) | copy-start | bytes 98308
  0.6 9.6 %copy-start.1 = (f32[32,2048]{1,0:T(8,128)S(1)}, f32[32,2048]{1,0:T(8,128)}, u32[]{:S(2)}) copy-start(f32[32,2048]{1,0:T(8,128)} %own.1) | copy-start | bytes 786436
  0.7 9.5 %collective-permute-start = (f32[32,2048]{1,0:T(8,128)}, f32[32,2048]{1,0:T(8,128)S(1)}, u32[]{:S(2)}, u32[]{:S(2)}) collective-permute-start(f32[32,2048]{1,0:T(8,128)} %own.1), channel_id=1, source_target_pairs={{0,16},{16,0},{1,17},{17,1},{2,18},{18,2},{3,19},{19,3},{4,20},{20... | collective-permute-start | bytes 786440 | tf_op jit(solution)/shard_map/ppermute | solution.py:486
  9.8 3.0 %collective-permute-start.2 = (bf16[16,128,128]{2,1,0:T(8,128)(2,1)S(1)}, bf16[16,128,128]{2,1,0:T(8,128)(2,1)S(1)}, u32[]{:S(2)}, u32[]{:S(2)}) collective-permute-start(bf16[16,128,128]{2,1,0:T(8,128)(2,1)S(1)} %get-tuple-element.16.give), channel_id=1, source_target_pairs={{0,1},{1,0},{2,3},{3,2},{4,5},{5,4},{6,7},{7,6},{8,9},{9,8},{10,11... | collective-permute-start | bytes 1572872 | tf_op jit(solution)/shard_map/ppermute | solution.py:490
  11.6 1.2 %collective-permute-start.1 = (f32[32,128]{1,0:T(8,128)S(1)}, f32[32,128]{1,0:T(8,128)S(1)}, u32[]{:S(2)}, u32[]{:S(2)}) collective-permute-start(f32[32,128]{1,0:T(8,128)S(1)} %get-tuple-element.17.acts), channel_id=1, source_target_pairs={{0,1},{1,0},{2,3},{3,2},{4,5},{5,4},{6,7},{7,6},{8,9},{9,8},{10,11... | collective-permute-start | bytes 49160 | tf_op jit(solution)/shard_map/ppermute | solution.py:512
  41.1 1.2 %collective-permute-start.3 = (f32[72,128]{1,0:T(8,128)S(1)}, f32[72,128]{1,0:T(8,128)S(1)}, u32[]{:S(2)}, u32[]{:S(2)}) collective-permute-start(f32[72,128]{1,0:T(8,128)S(1)} %partial.1.half), channel_id=1, source_target_pairs={{0,1},{1,0},{2,3},{3,2},{4,5},{5,4},{6,7},{7,6},{8,9},{9,8},{10,11... | collective-permute-start | bytes 110600 | tf_op jit(solution)/shard_map/ppermute | solution.py:520
  55.4 10.8 %all-to-all-start.3 = ((f16[32,16,128]{2,1,0:T(8,128)(2,1)}), f16[32,16,128]{2,1,0:T(8,128)(2,1)S(1)}, u32[]{:S(2)}, u32[]{:S(2)}) async-start(f16[32,16,128]{2,1,0:T(8,128)(2,1)} %bitcast.3), calls=%async_computation.3 | async-start | bytes 262144 | tf_op jit(solution)/shard_map/all_to_all | solution.py:496
  58.0 8.3 %collective-permute-start.4 = (f32[32,128]{1,0:T(8,128)S(1)}, f32[32,128]{1,0:T(8,128)S(1)}, u32[]{:S(2)}, u32[]{:S(2)}) collective-permute-start(f32[32,128]{1,0:T(8,128)S(1)} %get-tuple-element.27.acts), channel_id=1, source_target_pairs={{0,16},{16,0},{1,17},{17,1},{2,18},{18,2},{3,19},{19,3},{4,20},{20... | collective-permute-start | bytes 49160 | tf_op jit(solution)/shard_map/ppermute | solution.py:527
where the time goes:
time: 68.2 us; the launch traced here: 67.9 us
  blocking collectives  37.2 us (55%)
  Pallas kernels  12.4 us (18%)
  waiting for transfers between devices  8.81 us (13%)
  starting transfers between devices  7.77 us (11%)
  between operations  0.77 us (1%)
  local copies, waits for them, and re-layouts  0.72 us (1%)
    all_to_all x3, blocking collectives, exchange(): lax.all_to_all(value.astype(f16), axes, split_axis=0, concat_axis=0, tile...  37.2 us
    all_to_all x1, waiting for transfers between devices, exchange(): lax.all_to_all(value.astype(f16), axes, split_axis=0, concat_axis=0, tile...  6.51 us
    pallas_call x7, Pallas kernels, local(): pl.pallas_call(kernel, out_shape=shapes if many else shapes[0], in_specs=...  6.23 us
    pallas_call x1, Pallas kernels, spectrum(): pl.pallas_call(spectrum_kernel, out_shape=[jax.ShapeDtypeStruct((HALF //...  6.15 us
    ppermute x1, starting transfers between devices, row_shards(): other = lax.ppermute(w_start, 'freq', swap)  3.03 us
    all_to_all x1, starting transfers between devices, exchange(): lax.all_to_all(value.astype(f16), axes, split_axis=0, concat_axis=0, tile...  2.58 us
    ppermute x1, starting transfers between devices, row_shards(): partner = lax.ppermute(acts, 'freq', swap)  1.72 us
  transfers between devices with their start and end apart: 6, of which 4 were waited for; matrix products, arithmetic and copies ran while one was open for 0% of the time, Pallas kernels for 11%

commit v1 on v0

--- a/solution.py
+++ b/solution.py
@@ -378,16 +378,15 @@
     finish((acts[...], sibling[...]), (keep, taken), parts)
 
 
-def partial_kernel(got, keep, taken, peak, out):
-    comp = out.shape[0] - got.shape[1]
-    scales, gram = opened(got, comp)
-    wide = [(got[u, :comp, :] * scales[u]).astype(jnp.bfloat16) for u in range(SIDE)]
-    wide = jnp.concatenate(wide, axis=1)
+def partial_kernel(got, exps, keep, taken, peak, out):
+    comp = got.shape[1]
+    wide = jnp.concatenate([got[u] for u in range(SIDE)], axis=1) * power(exps[:, :1])
+    left = wide.astype(jnp.bfloat16)
     for k, grid in enumerate((keep, taken)):
         out[k * comp : (k + 1) * comp, :] = lax.dot_general(
-            wide, tall(grid), NT, preferred_element_type=jnp.float32
+            left, tall(grid), NT, preferred_element_type=jnp.float32
         )
-    packed = pack(gram)
+    packed = pack(gram_of(wide))
     rows, lanes = places(packed.shape)
     highest = jnp.max(peak[...].astype(jnp.float32), axis=(0, 1), keepdims=True)
     place = (rows == packed.shape[0] - 1) & (lanes == LANES - comp)
@@ -408,28 +407,41 @@
     finish((new, sibling_new), (keep, taken), parts, peak)
 
 
-def slice_kernel(got, mine, out, payload):
+def eleven_bits(value):
+    split = value * 8193.0
+    return split - (split - value)
+
+
+def rounded(value):
+    def short(x):
+        return x.astype(jnp.bfloat16).astype(jnp.float32)
+
+    near = eleven_bits(value)
+    step = jnp.abs(near) * 2.0**-10.6
+    moved = eleven_bits(near + jnp.where(value > near, step, -step))
+    return jnp.where(short(near) == short(value), near, moved)
+
+
+def slice_of(got, mine):
     comp = mine.shape[0]
     scales, gram = opened(got, comp)
     sums = sum(got[s, :comp, :] * scales[s] for s in range(got.shape[0]))
-    new = update(mine[...], sums, gram)
-    out[...] = new
-    gram = lax.dot_general(new, new, NT, precision=HIGHEST, preferred_element_type=jnp.float32)
-    squares = jnp.sum(new * new, axis=1, keepdims=True)
-    sums, packed = sealed(new.astype(jnp.bfloat16).astype(jnp.float32), gram, squares)
-    payload[:comp, :] = sums
-    payload[comp:, :] = packed
-
-
-def last_kernel(got, mine, out, exps_out):
-    comp = mine.shape[0]
-    scales, gram = opened(got, comp)
-    sums = sum(got[s, :comp, :] * scales[s] for s in range(got.shape[0]))
-    new = update(mine[...], sums, gram)
     at = places(gram.shape)
     diagonal = jnp.sum(jnp.where(at[0] == at[1], gram, 0.0), axis=1, keepdims=True)
     bound = sum(scales) * 2.0 ** (TOP + 1) / jnp.maximum(diagonal, 1e-30)
     exps = jnp.clip(jnp.floor(jnp.log2(jnp.maximum(bound, 1e-30))), -100, 100) - TOP
+    return update(mine[...], sums, gram), exps
+
+
+def slice_kernel(got, mine, out, payload, exps_out):
+    new, exps = slice_of(got, mine)
+    out[...] = new
+    payload[...] = rounded(new * power(-exps))
+    exps_out[...] = jnp.broadcast_to(exps, exps_out.shape)
+
+
+def last_kernel(got, mine, out, exps_out):
+    new, exps = slice_of(got, mine)
     exps_out[...] = jnp.broadcast_to(exps, exps_out.shape)
     turned = (new * power(-exps)).T
     span = OUTER // 4
@@ -513,10 +525,9 @@
     parts = local(sums_kernel, message, "sums", acts, sibling, keep, taken)
     for step in range(ITERS - 1):
         got = exchange(parts)
-        outs = [lane_rows, ((comp + extra, LANES), f32)]
-        mine, payload = local(slice_kernel, outs, "slice", got, mine)
+        mine, payload, exps = local(slice_kernel, [lane_rows] * 3, "slice", got, mine)
         got = exchange(jnp.broadcast_to(payload, (SIDE,) + payload.shape))
-        half = local(partial_kernel, ((2 * comp + extra, LANES), f32), "partial", got, keep, taken, peak)
+        half = local(partial_kernel, ((2 * comp + extra, LANES), f32), "partial", got, exps, keep, taken, peak)
         other_half = lax.ppermute(half, "core", swap)
         outs = [message, (acts.shape, f32)]
         parts, acts = local(

time: 68.2 us -> 67.8 us (level)
  no operation moved by 1% of the time
where the time goes in v1:
time: 67.8 us; the launch traced here: 67.6 us
  blocking collectives  37 us (55%)
  Pallas kernels  12.2 us (18%)
  waiting for transfers between devices  8.78 us (13%)
  starting transfers between devices  7.78 us (11%)
  between operations  0.78 us (1%)
  local copies, waits for them, and re-layouts  0.72 us (1%)
    all_to_all x3, blocking collectives, exchange(): lax.all_to_all(value.astype(f16), axes, split_axis=0, concat_axis=0, tile...  37 us
    all_to_all x1, waiting for transfers between devices, exchange(): lax.all_to_all(value.astype(f16), axes, split_axis=0, concat_axis=0, tile...  6.51 us
    pallas_call x1, Pallas kernels, spectrum(): pl.pallas_call(spectrum_kernel, out_shape=[jax.ShapeDtypeStruct((HALF //...  6.15 us
    pallas_call x7, Pallas kernels, local(): pl.pallas_call(kernel, out_shape=shapes if many else shapes[0], in_specs=...  6.1 us
    ppermute x1, starting transfers between devices, row_shards(): other = lax.ppermute(w_start, 'freq', swap)  3.03 us
    all_to_all x1, starting transfers between devices, exchange(): lax.all_to_all(value.astype(f16), axes, split_axis=0, concat_axis=0, tile...  2.58 us
    ppermute x1, starting transfers between devices, row_shards(): partner = lax.ppermute(acts, 'freq', swap)  1.72 us
  transfers between devices with their start and end apart: 6, of which 4 were waited for; matrix products, arithmetic and copies ran while one was open for 0% of the time, Pallas kernels for 11%

profile of v1, /device:TPU:0, one launch (start us, length us, event | category | flops | bytes accessed | tf_op | source)
XLA Modules:
  0.0 67.6 jit_solution(1230444347974181178)
XLA Ops:
  0.6 0.0 copy-start
  0.6 0.0 copy-start.1
  0.7 3.0 %collective-permute-start = (f32[32,2048]{1,0:T(8,128)}, f32[32,2048]{1,0:T(8,128)S(1)}, u32[]{:S(2)}, u32[]{:S(2)}) collective-permute-start(f32[32,2048]{1,0:T(8,128)} %own.1), channel_id=1, source_target_pairs={{0,16},{16,0},{1,17},{17,1},{2,18},{18,2},{3,19},{19,3},{4,20},{20... | collective-permute-start | bytes 786440 | tf_op jit(solution)/shard_map/ppermute | solution.py:498
  3.7 6.1 %spectrum.1 = (bf16[16,128,128]{2,1,0:T(8,128)(2,1)S(1)}, bf16[16,128,128]{2,1,0:T(8,128)(2,1)S(1)}, bf16[16,128]{1,0:T(8,128)(2,1)S(1)}) custom-call(s32[1]{0:T(128)} %bitcast.1.core, bf16[1,1048576]{1,0:T(2,128)(2,1)} %audio.1, f32[1216,128]{1,0:T(8,128)} %constant.24.clone.source), custom_call_target="tpu_custom_call" | custom-call | flops 2013265920 | bytes 4194304 | tf_op jit(solution)/shard_map/spectrum/pallas_call | solution.py:151
  9.8 0.1 collective-permute-start.2
  9.9 0.1 pad_add_fusion.at
  10.0 0.0 copy-done
  10.0 0.2 collective-permute-done.other
  10.2 0.0 copy-done.1
  10.2 1.4 %start.1 = (f32[32,128]{1,0:T(8,128)S(1)}, f32[32,128]{1,0:T(8,128)S(1)}) custom-call(s32[3]{0:T(128)S(1)} %pad_add_fusion.at, f32[32,2048]{1,0:T(8,128)S(1)} %copy-done.1, f32[32,2048]{1,0:T(8,128)S(1)} %collective-permute-done.other, bf16[16,128,128]{2,1,0:T(8,128)(2,1)S(1)} %get-tuple-element.16.keep, bf16[16,128,128]{2,1,0:T(8,128)(2,1)S(1)} %get-tuple-element.17.give, ...), custom_call_target="tpu_custom_call" | custom-call | flops 17179869184 | bytes 33554432 | tf_op jit(solution)/shard_map/start/pallas_call | solution.py:479
  11.6 0.4 collective-permute-start.1
  12.0 0.9 %collective-permute-done.1.sibling = f32[32,128]{1,0:T(8,128)S(1)} collective-permute-done((f32[32,128]{1,0:T(8,128)S(1)}, f32[32,128]{1,0:T(8,128)S(1)}, u32[]{:S(2)}, u32[]{:S(2)}) %collective-permute-start.1) | collective-permute-done | bytes 16416 | tf_op jit(solution)/shard_map/ppermute | solution.py:524
  12.8 0.0 collective-permute-done.2.taken
  12.9 0.5 sums.1
  13.4 15.0 %all_to_all.20 = f16[16,40,128]{2,1,0:T(8,128)(2,1)S(1)} all-to-all(f16[16,40,128]{2,1,0:T(8,128)(2,1)S(1)} %convert_element_type.29), channel_id=1, replica_groups=mesh['freq'=2,'chips'=8,'core'=2] {'freq','chips'}, dimensions={0} | all-to-all | bytes 327680 | tf_op jit(solution)/shard_map/all_to_all | solution.py:508
  28.5 0.5 slice.1
  29.0 11.0 %all_to_all.21 = f16[16,32,128]{2,1,0:T(8,128)(2,1)S(1)} all-to-all(f16[16,32,128]{2,1,0:T(8,128)(2,1)S(1)} %broadcast_in_dim.4), channel_id=1, replica_groups=mesh['freq'=2,'chips'=8,'core'=2] {'freq','chips'}, dimensions={0} | all-to-all | bytes 262144 | tf_op jit(solution)/shard_map/all_to_all | solution.py:508
  40.0 0.8 %partial.1.half = f32[72,128]{1,0:T(8,128)S(1)} custom-call(f32[16,32,128]{2,1,0:T(8,128)S(1)} %convert_element_type.32.got, f32[32,128]{1,0:T(8,128)S(1)} %get-tuple-element.21.exps, bf16[16,128,128]{2,1,0:T(8,128)(2,1)S(1)} %get-tuple-element.16.keep, bf16[16,128,128]{2,1,0:T(8,128)(2,1)S(1)} %collective-permute-done.2.taken, ...), custom_call_target="tpu_custom_call" | custom-call | tf_op jit(solution)/shard_map/partial/pallas_call | solution.py:479
  40.8 0.0 collective-permute-start.3
  40.8 1.2 %collective-permute-done.3.other_half = f32[72,128]{1,0:T(8,128)S(1)} collective-permute-done((f32[72,128]{1,0:T(8,128)S(1)}, f32[72,128]{1,0:T(8,128)S(1)}, u32[]{:S(2)}, u32[]{:S(2)}) %collective-permute-start.3) | collective-permute-done | bytes 36896 | tf_op jit(solution)/shard_map/ppermute | solution.py:531
  42.0 0.7 again.1
  42.7 11.0 %all_to_all.22 = f16[16,40,128]{2,1,0:T(8,128)(2,1)S(1)} all-to-all(f16[16,40,128]{2,1,0:T(8,128)(2,1)S(1)} %convert_element_type.33), channel_id=1, replica_groups=mesh['freq'=2,'chips'=8,'core'=2] {'freq','chips'}, dimensions={0} | all-to-all | bytes 327680 | tf_op jit(solution)/shard_map/all_to_all | solution.py:508
  53.8 0.7 last.1
  54.5 0.7 %broadcast_in_dim.10 = f16[2,16,16,128]{3,2,1,0:T(8,128)(2,1)} broadcast(f16[2,16,128]{2,1,0:T(8,128)(2,1)S(1)} %convert_element_type.35), dimensions={0,2,3} | broadcast | bytes 139264 | tf_op jit(solution)/shard_map/broadcast_in_dim | solution.py:540
  55.1 2.6 %all-to-all-start.3 = ((f16[32,16,128]{2,1,0:T(8,128)(2,1)}), f16[32,16,128]{2,1,0:T(8,128)(2,1)S(1)}, u32[]{:S(2)}, u32[]{:S(2)}) async-start(f16[32,16,128]{2,1,0:T(8,128)(2,1)} %bitcast.3), calls=%async_computation.3 | async-start | bytes 262144 | tf_op jit(solution)/shard_map/all_to_all | solution.py:508
  57.7 1.7 %collective-permute-start.4 = (f32[32,128]{1,0:T(8,128)S(1)}, f32[32,128]{1,0:T(8,128)S(1)}, u32[]{:S(2)}, u32[]{:S(2)}) collective-permute-start(f32[32,128]{1,0:T(8,128)S(1)} %get-tuple-element.29.acts), channel_id=1, source_target_pairs={{0,16},{16,0},{1,17},{17,1},{2,18},{18,2},{3,19},{19,3},{4,20},{20... | collective-permute-start | bytes 49160 | tf_op jit(solution)/shard_map/ppermute | solution.py:538
  59.5 6.5 %all-to-all-done.3 = f16[32,16,128]{2,1,0:T(8,128)(2,1)S(1)} async-done(((f16[32,16,128]{2,1,0:T(8,128)(2,1)}), f16[32,16,128]{2,1,0:T(8,128)(2,1)S(1)}, u32[]{:S(2)}, u32[]{:S(2)}) %all-to-all-start.3) | async-done | bytes 131104 | tf_op jit(solution)/shard_map/all_to_all | solution.py:508
  66.0 0.0 collective-permute-done.4.partner
  66.0 1.6 %natural.1 = (f32[32,2048]{1,0:T(8,128)}, f32[32,256]{1,0:T(8,128)}) custom-call(s32[3]{0:T(128)S(1)} %pad_add_fusion.at, f32[32,16,128]{2,1,0:T(8,128)S(1)} %convert_element_type.37.got, f32[32,128]{1,0:T(8,128)S(1)} %get-tuple-element.28.exps, f32[32,128]{1,0:T(8,128)S(1)} %get-tuple-element.29.acts, f32[32,128]{1,0:T(8,128)S(1)} %collective-permute-done.4.partner), custom_call_target="tpu_custom_call" | custom-call | tf_op jit(solution)/shard_map/natural/pallas_call | solution.py:479
  (10 shorter events, 0.2 us)
Async XLA Ops:
  0.6 9.4 %copy-start = (f32[32,256]{1,0:T(8,128)S(1)}, f32[32,256]{1,0:T(8,128)}, u32[]{:S(2)}) copy-start(f32[32,256]{1,0:T(8,128)} %param.6) | copy-start | bytes 98308
  0.6 9.6 %copy-start.1 = (f32[32,2048]{1,0:T(8,128)S(1)}, f32[32,2048]{1,0:T(8,128)}, u32[]{:S(2)}) copy-start(f32[32,2048]{1,0:T(8,128)} %own.1) | copy-start | bytes 786436
  0.7 9.5 %collective-permute-start = (f32[32,2048]{1,0:T(8,128)}, f32[32,2048]{1,0:T(8,128)S(1)}, u32[]{:S(2)}, u32[]{:S(2)}) collective-permute-start(f32[32,2048]{1,0:T(8,128)} %own.1), channel_id=1, source_target_pairs={{0,16},{16,0},{1,17},{17,1},{2,18},{18,2},{3,19},{19,3},{4,20},{20... | collective-permute-start | bytes 786440 | tf_op jit(solution)/shard_map/ppermute | solution.py:498
  9.8 3.0 %collective-permute-start.2 = (bf16[16,128,128]{2,1,0:T(8,128)(2,1)S(1)}, bf16[16,128,128]{2,1,0:T(8,128)(2,1)S(1)}, u32[]{:S(2)}, u32[]{:S(2)}) collective-permute-start(bf16[16,128,128]{2,1,0:T(8,128)(2,1)S(1)} %get-tuple-element.17.give), channel_id=1, source_target_pairs={{0,1},{1,0},{2,3},{3,2},{4,5},{5,4},{6,7},{7,6},{8,9},{9,8},{10,11... | collective-permute-start | bytes 1572872 | tf_op jit(solution)/shard_map/ppermute | solution.py:502
  11.6 1.2 %collective-permute-start.1 = (f32[32,128]{1,0:T(8,128)S(1)}, f32[32,128]{1,0:T(8,128)S(1)}, u32[]{:S(2)}, u32[]{:S(2)}) collective-permute-start(f32[32,128]{1,0:T(8,128)S(1)} %get-tuple-element.18.acts), channel_id=1, source_target_pairs={{0,1},{1,0},{2,3},{3,2},{4,5},{5,4},{6,7},{7,6},{8,9},{9,8},{10,11... | collective-permute-start | bytes 49160 | tf_op jit(solution)/shard_map/ppermute | solution.py:524
  40.8 1.2 %collective-permute-start.3 = (f32[72,128]{1,0:T(8,128)S(1)}, f32[72,128]{1,0:T(8,128)S(1)}, u32[]{:S(2)}, u32[]{:S(2)}) collective-permute-start(f32[72,128]{1,0:T(8,128)S(1)} %partial.1.half), channel_id=1, source_target_pairs={{0,1},{1,0},{2,3},{3,2},{4,5},{5,4},{6,7},{7,6},{8,9},{9,8},{10,11... | collective-permute-start | bytes 110600 | tf_op jit(solution)/shard_map/ppermute | solution.py:531
  55.1 10.8 %all-to-all-start.3 = ((f16[32,16,128]{2,1,0:T(8,128)(2,1)}), f16[32,16,128]{2,1,0:T(8,128)(2,1)S(1)}, u32[]{:S(2)}, u32[]{:S(2)}) async-start(f16[32,16,128]{2,1,0:T(8,128)(2,1)} %bitcast.3), calls=%async_computation.3 | async-start | bytes 262144 | tf_op jit(solution)/shard_map/all_to_all | solution.py:508
  57.7 8.3 %collective-permute-start.4 = (f32[32,128]{1,0:T(8,128)S(1)}, f32[32,128]{1,0:T(8,128)S(1)}, u32[]{:S(2)}, u32[]{:S(2)}) collective-permute-start(f32[32,128]{1,0:T(8,128)S(1)} %get-tuple-element.29.acts), channel_id=1, source_target_pairs={{0,16},{16,0},{1,17},{17,1},{2,18},{18,2},{3,19},{19,3},{4,20},{20... | collective-permute-start | bytes 49160 | tf_op jit(solution)/shard_map/ppermute | solution.py:538

commit v2 on v1

--- a/solution.py
+++ b/solution.py
@@ -361,12 +361,13 @@
 
 def finish(acts, grids, parts, peak=None):
     comp = acts[0].shape[0]
-    sums, gram, weight, squares = 0.0, 0.0, 0.0, 0.0
-    for value, grid in zip(acts, grids):
-        left = value.astype(jnp.bfloat16)
-        weight += jnp.sum(left.astype(jnp.float32), axis=1, keepdims=True)
+    left = [value.astype(jnp.bfloat16) for value in acts]
+    both = jnp.concatenate([tall(grid) for grid in grids], axis=0)
+    sums = jnp.dot(jnp.concatenate(left, axis=1), both, preferred_element_type=jnp.float32)
+    gram, weight, squares = 0.0, 0.0, 0.0
+    for value, short in zip(acts, left):
+        weight += jnp.sum(short.astype(jnp.float32), axis=1, keepdims=True)
         squares += jnp.sum(value * value, axis=1, keepdims=True)
-        sums += jnp.dot(left, tall(grid), preferred_element_type=jnp.float32)
         gram += lax.dot_general(value, value, NT, precision=HIGHEST, preferred_element_type=jnp.float32)
     sums, packed = sealed(sums, gram, squares, None if peak is None else weight * (1.01 * peak))
     for u in range(SIDE):
@@ -382,10 +383,10 @@
     comp = got.shape[1]
     wide = jnp.concatenate([got[u] for u in range(SIDE)], axis=1) * power(exps[:, :1])
     left = wide.astype(jnp.bfloat16)
-    for k, grid in enumerate((keep, taken)):
-        out[k * comp : (k + 1) * comp, :] = lax.dot_general(
-            left, tall(grid), NT, preferred_element_type=jnp.float32
-        )
+    both = jnp.concatenate([tall(keep), tall(taken)], axis=0)
+    numer = lax.dot_general(left, both, NT, preferred_element_type=jnp.float32)
+    for k in range(2):
+        out[k * comp : (k + 1) * comp, :] = numer[:, k * LANES : (k + 1) * LANES]
     packed = pack(gram_of(wide))
     rows, lanes = places(packed.shape)
     highest = jnp.max(peak[...].astype(jnp.float32), axis=(0, 1), keepdims=True)

time: 67.8 us -> 67.8 us (level)
  no operation moved by 1% of the time
where the time goes in v2:
time: 67.8 us; the launch traced here: 67.5 us
  blocking collectives  37 us (55%)
  Pallas kernels  12.2 us (18%)
  waiting for transfers between devices  8.78 us (13%)
  starting transfers between devices  7.78 us (11%)
  between operations  0.78 us (1%)
  local copies, waits for them, and re-layouts  0.72 us (1%)
    all_to_all x3, blocking collectives, exchange(): lax.all_to_all(value.astype(f16), axes, split_axis=0, concat_axis=0, tile...  37 us
    all_to_all x1, waiting for transfers between devices, exchange(): lax.all_to_all(value.astype(f16), axes, split_axis=0, concat_axis=0, tile...  6.51 us
    pallas_call x1, Pallas kernels, spectrum(): pl.pallas_call(spectrum_kernel, out_shape=[jax.ShapeDtypeStruct((HALF //...  6.15 us
    pallas_call x7, Pallas kernels, local(): pl.pallas_call(kernel, out_shape=shapes if many else shapes[0], in_specs=...  6.02 us
    ppermute x1, starting transfers between devices, row_shards(): other = lax.ppermute(w_start, 'freq', swap)  3.03 us
    all_to_all x1, starting transfers between devices, exchange(): lax.all_to_all(value.astype(f16), axes, split_axis=0, concat_axis=0, tile...  2.58 us
    ppermute x1, starting transfers between devices, row_shards(): partner = lax.ppermute(acts, 'freq', swap)  1.72 us
  transfers between devices with their start and end apart: 6, of which 4 were waited for; matrix products, arithmetic and copies ran while one was open for 0% of the time, Pallas kernels for 11%

profile of v2, /device:TPU:0, one launch (start us, length us, event | category | flops | bytes accessed | tf_op | source)
XLA Modules:
  0.0 67.5 jit_solution(13807869383823982139)
XLA Ops:
  0.6 0.0 copy-start
  0.6 0.0 copy-start.1
  0.7 3.0 %collective-permute-start = (f32[32,2048]{1,0:T(8,128)}, f32[32,2048]{1,0:T(8,128)S(1)}, u32[]{:S(2)}, u32[]{:S(2)}) collective-permute-start(f32[32,2048]{1,0:T(8,128)} %own.1), channel_id=1, source_target_pairs={{0,16},{16,0},{1,17},{17,1},{2,18},{18,2},{3,19},{19,3},{4,20},{20... | collective-permute-start | bytes 786440 | tf_op jit(solution)/shard_map/ppermute | solution.py:499
  3.7 6.1 %spectrum.1 = (bf16[16,128,128]{2,1,0:T(8,128)(2,1)S(1)}, bf16[16,128,128]{2,1,0:T(8,128)(2,1)S(1)}, bf16[16,128]{1,0:T(8,128)(2,1)S(1)}) custom-call(s32[1]{0:T(128)} %bitcast.1.core, bf16[1,1048576]{1,0:T(2,128)(2,1)} %audio.1, f32[1216,128]{1,0:T(8,128)} %constant.24.clone.source), custom_call_target="tpu_custom_call" | custom-call | flops 2013265920 | bytes 4194304 | tf_op jit(solution)/shard_map/spectrum/pallas_call | solution.py:151
  9.8 0.1 collective-permute-start.2
  9.9 0.1 pad_add_fusion.at
  10.0 0.0 copy-done
  10.0 0.2 collective-permute-done.other
  10.2 0.0 copy-done.1
  10.2 1.4 %start.1 = (f32[32,128]{1,0:T(8,128)S(1)}, f32[32,128]{1,0:T(8,128)S(1)}) custom-call(s32[3]{0:T(128)S(1)} %pad_add_fusion.at, f32[32,2048]{1,0:T(8,128)S(1)} %copy-done.1, f32[32,2048]{1,0:T(8,128)S(1)} %collective-permute-done.other, bf16[16,128,128]{2,1,0:T(8,128)(2,1)S(1)} %get-tuple-element.16.keep, bf16[16,128,128]{2,1,0:T(8,128)(2,1)S(1)} %get-tuple-element.17.give, ...), custom_call_target="tpu_custom_call" | custom-call | flops 17179869184 | bytes 33554432 | tf_op jit(solution)/shard_map/start/pallas_call | solution.py:480
  11.6 0.4 collective-permute-start.1
  12.0 0.9 %collective-permute-done.1.sibling = f32[32,128]{1,0:T(8,128)S(1)} collective-permute-done((f32[32,128]{1,0:T(8,128)S(1)}, f32[32,128]{1,0:T(8,128)S(1)}, u32[]{:S(2)}, u32[]{:S(2)}) %collective-permute-start.1) | collective-permute-done | bytes 16416 | tf_op jit(solution)/shard_map/ppermute | solution.py:525
  12.8 0.0 collective-permute-done.2.taken
  12.9 0.5 sums.1
  13.4 15.1 %all_to_all.20 = f16[16,40,128]{2,1,0:T(8,128)(2,1)S(1)} all-to-all(f16[16,40,128]{2,1,0:T(8,128)(2,1)S(1)} %convert_element_type.29), channel_id=1, replica_groups=mesh['freq'=2,'chips'=8,'core'=2] {'freq','chips'}, dimensions={0} | all-to-all | bytes 327680 | tf_op jit(solution)/shard_map/all_to_all | solution.py:509
  28.5 0.5 slice.1
  29.0 11.0 %all_to_all.21 = f16[16,32,128]{2,1,0:T(8,128)(2,1)S(1)} all-to-all(f16[16,32,128]{2,1,0:T(8,128)(2,1)S(1)} %broadcast_in_dim.4), channel_id=1, replica_groups=mesh['freq'=2,'chips'=8,'core'=2] {'freq','chips'}, dimensions={0} | all-to-all | bytes 262144 | tf_op jit(solution)/shard_map/all_to_all | solution.py:509
  40.0 0.7 %partial.1.half = f32[72,128]{1,0:T(8,128)S(1)} custom-call(f32[16,32,128]{2,1,0:T(8,128)S(1)} %convert_element_type.32.got, f32[32,128]{1,0:T(8,128)S(1)} %get-tuple-element.21.exps, bf16[16,128,128]{2,1,0:T(8,128)(2,1)S(1)} %get-tuple-element.16.keep, bf16[16,128,128]{2,1,0:T(8,128)(2,1)S(1)} %collective-permute-done.2.taken, ...), custom_call_target="tpu_custom_call" | custom-call | tf_op jit(solution)/shard_map/partial/pallas_call | solution.py:480
  40.7 0.0 collective-permute-start.3
  40.8 1.2 %collective-permute-done.3.other_half = f32[72,128]{1,0:T(8,128)S(1)} collective-permute-done((f32[72,128]{1,0:T(8,128)S(1)}, f32[72,128]{1,0:T(8,128)S(1)}, u32[]{:S(2)}, u32[]{:S(2)}) %collective-permute-start.3) | collective-permute-done | bytes 36896 | tf_op jit(solution)/shard_map/ppermute | solution.py:532
  42.0 0.6 again.1
  42.6 11.0 %all_to_all.22 = f16[16,40,128]{2,1,0:T(8,128)(2,1)S(1)} all-to-all(f16[16,40,128]{2,1,0:T(8,128)(2,1)S(1)} %convert_element_type.33), channel_id=1, replica_groups=mesh['freq'=2,'chips'=8,'core'=2] {'freq','chips'}, dimensions={0} | all-to-all | bytes 327680 | tf_op jit(solution)/shard_map/all_to_all | solution.py:509
  53.7 0.7 last.1
  54.4 0.7 %broadcast_in_dim.10 = f16[2,16,16,128]{3,2,1,0:T(8,128)(2,1)} broadcast(f16[2,16,128]{2,1,0:T(8,128)(2,1)S(1)} %convert_element_type.35), dimensions={0,2,3} | broadcast | bytes 139264 | tf_op jit(solution)/shard_map/broadcast_in_dim | solution.py:541
  55.1 2.6 %all-to-all-start.3 = ((f16[32,16,128]{2,1,0:T(8,128)(2,1)}), f16[32,16,128]{2,1,0:T(8,128)(2,1)S(1)}, u32[]{:S(2)}, u32[]{:S(2)}) async-start(f16[32,16,128]{2,1,0:T(8,128)(2,1)} %bitcast.3), calls=%async_computation.3 | async-start | bytes 262144 | tf_op jit(solution)/shard_map/all_to_all | solution.py:509
  57.7 1.7 %collective-permute-start.4 = (f32[32,128]{1,0:T(8,128)S(1)}, f32[32,128]{1,0:T(8,128)S(1)}, u32[]{:S(2)}, u32[]{:S(2)}) collective-permute-start(f32[32,128]{1,0:T(8,128)S(1)} %get-tuple-element.29.acts), channel_id=1, source_target_pairs={{0,16},{16,0},{1,17},{17,1},{2,18},{18,2},{3,19},{19,3},{4,20},{20... | collective-permute-start | bytes 49160 | tf_op jit(solution)/shard_map/ppermute | solution.py:539
  59.4 6.5 %all-to-all-done.3 = f16[32,16,128]{2,1,0:T(8,128)(2,1)S(1)} async-done(((f16[32,16,128]{2,1,0:T(8,128)(2,1)}), f16[32,16,128]{2,1,0:T(8,128)(2,1)S(1)}, u32[]{:S(2)}, u32[]{:S(2)}) %all-to-all-start.3) | async-done | bytes 131104 | tf_op jit(solution)/shard_map/all_to_all | solution.py:509
  65.9 0.0 collective-permute-done.4.partner
  65.9 1.6 %natural.1 = (f32[32,2048]{1,0:T(8,128)}, f32[32,256]{1,0:T(8,128)}) custom-call(s32[3]{0:T(128)S(1)} %pad_add_fusion.at, f32[32,16,128]{2,1,0:T(8,128)S(1)} %convert_element_type.37.got, f32[32,128]{1,0:T(8,128)S(1)} %get-tuple-element.28.exps, f32[32,128]{1,0:T(8,128)S(1)} %get-tuple-element.29.acts, f32[32,128]{1,0:T(8,128)S(1)} %collective-permute-done.4.partner), custom_call_target="tpu_custom_call" | custom-call | tf_op jit(solution)/shard_map/natural/pallas_call | solution.py:480
  (10 shorter events, 0.2 us)
Async XLA Ops:
  0.6 9.4 %copy-start = (f32[32,256]{1,0:T(8,128)S(1)}, f32[32,256]{1,0:T(8,128)}, u32[]{:S(2)}) copy-start(f32[32,256]{1,0:T(8,128)} %param.6) | copy-start | bytes 98308
  0.6 9.6 %copy-start.1 = (f32[32,2048]{1,0:T(8,128)S(1)}, f32[32,2048]{1,0:T(8,128)}, u32[]{:S(2)}) copy-start(f32[32,2048]{1,0:T(8,128)} %own.1) | copy-start | bytes 786436
  0.7 9.5 %collective-permute-start = (f32[32,2048]{1,0:T(8,128)}, f32[32,2048]{1,0:T(8,128)S(1)}, u32[]{:S(2)}, u32[]{:S(2)}) collective-permute-start(f32[32,2048]{1,0:T(8,128)} %own.1), channel_id=1, source_target_pairs={{0,16},{16,0},{1,17},{17,1},{2,18},{18,2},{3,19},{19,3},{4,20},{20... | collective-permute-start | bytes 786440 | tf_op jit(solution)/shard_map/ppermute | solution.py:499
  9.8 3.0 %collective-permute-start.2 = (bf16[16,128,128]{2,1,0:T(8,128)(2,1)S(1)}, bf16[16,128,128]{2,1,0:T(8,128)(2,1)S(1)}, u32[]{:S(2)}, u32[]{:S(2)}) collective-permute-start(bf16[16,128,128]{2,1,0:T(8,128)(2,1)S(1)} %get-tuple-element.17.give), channel_id=1, source_target_pairs={{0,1},{1,0},{2,3},{3,2},{4,5},{5,4},{6,7},{7,6},{8,9},{9,8},{10,11... | collective-permute-start | bytes 1572872 | tf_op jit(solution)/shard_map/ppermute | solution.py:503
  11.6 1.2 %collective-permute-start.1 = (f32[32,128]{1,0:T(8,128)S(1)}, f32[32,128]{1,0:T(8,128)S(1)}, u32[]{:S(2)}, u32[]{:S(2)}) collective-permute-start(f32[32,128]{1,0:T(8,128)S(1)} %get-tuple-element.18.acts), channel_id=1, source_target_pairs={{0,1},{1,0},{2,3},{3,2},{4,5},{5,4},{6,7},{7,6},{8,9},{9,8},{10,11... | collective-permute-start | bytes 49160 | tf_op jit(solution)/shard_map/ppermute | solution.py:525
  40.7 1.2 %collective-permute-start.3 = (f32[72,128]{1,0:T(8,128)S(1)}, f32[72,128]{1,0:T(8,128)S(1)}, u32[]{:S(2)}, u32[]{:S(2)}) collective-permute-start(f32[72,128]{1,0:T(8,128)S(1)} %partial.1.half), channel_id=1, source_target_pairs={{0,1},{1,0},{2,3},{3,2},{4,5},{5,4},{6,7},{7,6},{8,9},{9,8},{10,11... | collective-permute-start | bytes 110600 | tf_op jit(solution)/shard_map/ppermute | solution.py:532
  55.1 10.8 %all-to-all-start.3 = ((f16[32,16,128]{2,1,0:T(8,128)(2,1)}), f16[32,16,128]{2,1,0:T(8,128)(2,1)S(1)}, u32[]{:S(2)}, u32[]{:S(2)}) async-start(f16[32,16,128]{2,1,0:T(8,128)(2,1)} %bitcast.3), calls=%async_computation.3 | async-start | bytes 262144 | tf_op jit(solution)/shard_map/all_to_all | solution.py:509
  57.7 8.3 %collective-permute-start.4 = (f32[32,128]{1,0:T(8,128)S(1)}, f32[32,128]{1,0:T(8,128)S(1)}, u32[]{:S(2)}, u32[]{:S(2)}) collective-permute-start(f32[32,128]{1,0:T(8,128)S(1)} %get-tuple-element.29.acts), channel_id=1, source_target_pairs={{0,16},{16,0},{1,17},{17,1},{2,18},{18,2},{3,19},{19,3},{4,20},{20... | collective-permute-start | bytes 49160 | tf_op jit(solution)/shard_map/ppermute | solution.py:539

commit v3 on v2

--- a/solution.py
+++ b/solution.py
@@ -451,7 +451,7 @@
         out[freq] = jnp.concatenate([turned[a : a + span] for a in starts], axis=1)
 
 
-def natural_kernel(at, got, exps, acts, partner, out, acts_out, low, high):
+def natural_kernel(got, exps, out, low, high):
     comp = out.shape[0]
     span = OUTER // 4
     for r in range(HALF):
@@ -468,8 +468,6 @@
         for half in range(2):
             begin = (half * (span // 2) + pair) * LANES
             out[:, begin : begin + LANES] = turned[half * comp : (half + 1) * comp] * factor
-    first, own, other = at[2] == 0, acts[...], partner[...]
-    acts_out[...] = jnp.concatenate([jnp.where(first, own, other), jnp.where(first, other, own)], axis=1)
 
 
 def local(kernel, outs, name, *arrays, scratch=(), cost=None):
@@ -540,17 +538,17 @@
     final, exps = local(last_kernel, [((2, OUTER // 4, LANES), f32), lane_rows], "last", got, mine)
     final = jnp.broadcast_to(final[:, None], (2, HALF // 2) + final.shape[1:])
     got = exchange(final.reshape((HALF,) + final.shape[2:]), ("freq", "chips", "core"))
-    return local(
+    components = local(
         natural_kernel,
-        [(w_start.shape, f32), (h_start.shape, f32)],
+        (w_start.shape, f32),
         "natural",
-        at,
         got,
         exps,
-        acts,
-        partner,
         scratch=[pltpu.VMEM((OUTER // 4 * (HALF + 1), LANES), f32)] * 2,
     )
+    first = freq_at == 0
+    halves_of = [jnp.where(first, acts, partner), jnp.where(first, partner, acts)]
+    return components, jnp.concatenate(halves_of, axis=1)
 
 
 def shards(n_freq, n_tm, audio, w_start, h_start):

time: 67.8 us -> 68.5 us (1.010)
  waiting for transfers between devices: 8.78 us -> 9.85 us
    all_to_all x1, waiting for transfers between devices: 6.51 us -> 7.58 us  [exchange(): lax.all_to_all(value.astype(f16), axes, split_axis=0, concat_axis=0, tile...]
    ppermute x1, starting transfers between devices: 1.72 us -> 0.96 us  [row_shards(): partner = lax.ppermute(acts, 'freq', swap)]
  transfers between devices with their start and end apart: 6 -> 6, of which waited for: 4 -> 4; matrix products, arithmetic and copies ran while one was open for 0% -> 2% of each run, Pallas kernels for 11% -> 12%
where the time goes in v3:
time: 68.5 us; the launch traced here: 68.2 us
  blocking collectives  37 us (54%)
  Pallas kernels  11.6 us (17%)
  waiting for transfers between devices  9.85 us (14%)
  starting transfers between devices  7.32 us (11%)
  other arithmetic  0.85 us (1%)
  between operations  0.79 us (1%)
  local copies, waits for them, and re-layouts  0.72 us (1%)
    all_to_all x3, blocking collectives, exchange(): lax.all_to_all(value.astype(f16), axes, split_axis=0, concat_axis=0, tile...  37 us
    all_to_all x1, waiting for transfers between devices, exchange(): lax.all_to_all(value.astype(f16), axes, split_axis=0, concat_axis=0, tile...  7.58 us
    pallas_call x1, Pallas kernels, spectrum(): pl.pallas_call(spectrum_kernel, out_shape=[jax.ShapeDtypeStruct((HALF //...  6.15 us
    pallas_call x7, Pallas kernels, local(): pl.pallas_call(kernel, out_shape=shapes if many else shapes[0], in_specs=...  5.48 us
    ppermute x1, starting transfers between devices, row_shards(): other = lax.ppermute(w_start, 'freq', swap)  3.03 us
    all_to_all x1, starting transfers between devices, exchange(): lax.all_to_all(value.astype(f16), axes, split_axis=0, concat_axis=0, tile...  2.88 us
  transfers between devices with their start and end apart: 6, of which 4 were waited for; matrix products, arithmetic and copies ran while one was open for 2% of the time, Pallas kernels for 12%

profile of v3, /device:TPU:0, one launch (start us, length us, event | category | flops | bytes accessed | tf_op | source)
XLA Modules:
  0.0 68.2 jit_solution(10599627273262566252)
XLA Ops:
  0.6 0.0 copy-start
  0.6 0.0 copy-start.1
  0.7 3.0 %collective-permute-start = (f32[32,2048]{1,0:T(8,128)}, f32[32,2048]{1,0:T(8,128)S(1)}, u32[]{:S(2)}, u32[]{:S(2)}) collective-permute-start(f32[32,2048]{1,0:T(8,128)} %own.1), channel_id=1, source_target_pairs={{0,16},{16,0},{1,17},{17,1},{2,18},{18,2},{3,19},{19,3},{4,20},{20... | collective-permute-start | bytes 786440 | tf_op jit(solution)/shard_map/ppermute | solution.py:497
  3.7 6.1 %spectrum.1 = (bf16[16,128,128]{2,1,0:T(8,128)(2,1)S(1)}, bf16[16,128,128]{2,1,0:T(8,128)(2,1)S(1)}, bf16[16,128]{1,0:T(8,128)(2,1)S(1)}) custom-call(s32[1]{0:T(128)} %bitcast.1.core, bf16[1,1048576]{1,0:T(2,128)(2,1)} %audio.1, f32[1216,128]{1,0:T(8,128)} %constant.24.clone.source), custom_call_target="tpu_custom_call" | custom-call | flops 2013265920 | bytes 4194304 | tf_op jit(solution)/shard_map/spectrum/pallas_call | solution.py:151
  9.8 0.1 collective-permute-start.2
  9.9 0.1 pad_add_fusion.at
  10.0 0.0 copy-done
  10.0 0.2 collective-permute-done.other
  10.2 0.0 copy-done.1
  10.2 1.4 %start.1 = (f32[32,128]{1,0:T(8,128)S(1)}, f32[32,128]{1,0:T(8,128)S(1)}) custom-call(s32[3]{0:T(128)S(1)} %pad_add_fusion.at, f32[32,2048]{1,0:T(8,128)S(1)} %copy-done.1, f32[32,2048]{1,0:T(8,128)S(1)} %collective-permute-done.other, bf16[16,128,128]{2,1,0:T(8,128)(2,1)S(1)} %get-tuple-element.16.keep, bf16[16,128,128]{2,1,0:T(8,128)(2,1)S(1)} %get-tuple-element.17.give, ...), custom_call_target="tpu_custom_call" | custom-call | flops 17179869184 | bytes 33554432 | tf_op jit(solution)/shard_map/start/pallas_call | solution.py:478
  11.6 0.4 collective-permute-start.1
  12.0 0.9 %collective-permute-done.1.sibling = f32[32,128]{1,0:T(8,128)S(1)} collective-permute-done((f32[32,128]{1,0:T(8,128)S(1)}, f32[32,128]{1,0:T(8,128)S(1)}, u32[]{:S(2)}, u32[]{:S(2)}) %collective-permute-start.1) | collective-permute-done | bytes 16416 | tf_op jit(solution)/shard_map/ppermute | solution.py:523
  12.8 0.0 collective-permute-done.2.taken
  12.9 0.5 sums.1
  13.4 15.1 %all_to_all.20 = f16[16,40,128]{2,1,0:T(8,128)(2,1)S(1)} all-to-all(f16[16,40,128]{2,1,0:T(8,128)(2,1)S(1)} %convert_element_type.29), channel_id=1, replica_groups=mesh['freq'=2,'chips'=8,'core'=2] {'freq','chips'}, dimensions={0} | all-to-all | bytes 327680 | tf_op jit(solution)/shard_map/all_to_all | solution.py:507
  28.5 0.5 slice.1
  29.0 11.0 %all_to_all.21 = f16[16,32,128]{2,1,0:T(8,128)(2,1)S(1)} all-to-all(f16[16,32,128]{2,1,0:T(8,128)(2,1)S(1)} %broadcast_in_dim.4), channel_id=1, replica_groups=mesh['freq'=2,'chips'=8,'core'=2] {'freq','chips'}, dimensions={0} | all-to-all | bytes 262144 | tf_op jit(solution)/shard_map/all_to_all | solution.py:507
  40.0 0.7 %partial.1.half = f32[72,128]{1,0:T(8,128)S(1)} custom-call(f32[16,32,128]{2,1,0:T(8,128)S(1)} %convert_element_type.32.got, f32[32,128]{1,0:T(8,128)S(1)} %get-tuple-element.21.exps, bf16[16,128,128]{2,1,0:T(8,128)(2,1)S(1)} %get-tuple-element.16.keep, bf16[16,128,128]{2,1,0:T(8,128)(2,1)S(1)} %collective-permute-done.2.taken, ...), custom_call_target="tpu_custom_call" | custom-call | tf_op jit(solution)/shard_map/partial/pallas_call | solution.py:478
  40.7 0.0 collective-permute-start.3
  40.8 1.2 %collective-permute-done.3.other_half = f32[72,128]{1,0:T(8,128)S(1)} collective-permute-done((f32[72,128]{1,0:T(8,128)S(1)}, f32[72,128]{1,0:T(8,128)S(1)}, u32[]{:S(2)}, u32[]{:S(2)}) %collective-permute-start.3) | collective-permute-done | bytes 36896 | tf_op jit(solution)/shard_map/ppermute | solution.py:530
  42.0 0.6 again.1
  42.6 11.0 %all_to_all.22 = f16[16,40,128]{2,1,0:T(8,128)(2,1)S(1)} all-to-all(f16[16,40,128]{2,1,0:T(8,128)(2,1)S(1)} %convert_element_type.33), channel_id=1, replica_groups=mesh['freq'=2,'chips'=8,'core'=2] {'freq','chips'}, dimensions={0} | all-to-all | bytes 327680 | tf_op jit(solution)/shard_map/all_to_all | solution.py:507
  53.7 1.0 %collective-permute-start.4 = (f32[32,128]{1,0:T(8,128)S(1)}, f32[32,128]{1,0:T(8,128)S(1)}, u32[]{:S(2)}, u32[]{:S(2)}) collective-permute-start(f32[32,128]{1,0:T(8,128)S(1)} %get-tuple-element.29), channel_id=1, source_target_pairs={{0,16},{16,0},{1,17},{17,1},{2,18},{18,2},{3,19},{19,3},{4,20},{20... | collective-permute-start | bytes 49160 | tf_op jit(solution)/shard_map/ppermute | solution.py:537
  54.7 0.7 last.1
  55.4 0.7 broadcast_in_dim.10
  56.0 2.9 %all-to-all-start.3 = ((f16[32,16,128]{2,1,0:T(8,128)(2,1)}), f16[32,16,128]{2,1,0:T(8,128)(2,1)S(1)}, u32[]{:S(2)}, u32[]{:S(2)}) async-start(f16[32,16,128]{2,1,0:T(8,128)(2,1)} %bitcast.3), calls=%async_computation.3 | async-start | bytes 262144 | tf_op jit(solution)/shard_map/all_to_all | solution.py:507
  58.9 0.0 collective-permute-done.4
  58.9 0.6 pad_maximum_fusion
  59.6 7.6 %all-to-all-done.3 = f16[32,16,128]{2,1,0:T(8,128)(2,1)S(1)} async-done(((f16[32,16,128]{2,1,0:T(8,128)(2,1)}), f16[32,16,128]{2,1,0:T(8,128)(2,1)S(1)}, u32[]{:S(2)}, u32[]{:S(2)}) %all-to-all-start.3) | async-done | bytes 131104 | tf_op jit(solution)/shard_map/all_to_all | solution.py:507
  67.2 1.0 %natural.1 = f32[32,2048]{1,0:T(8,128)} custom-call(f32[32,16,128]{2,1,0:T(8,128)S(1)} %convert_element_type.37.got, f32[32,128]{1,0:T(8,128)S(1)} %get-tuple-element.28.exps), custom_call_target="tpu_custom_call" | custom-call | tf_op jit(solution)/shard_map/natural/pallas_call | solution.py:478
  (11 shorter events, 0.2 us)
Async XLA Ops:
  0.6 9.4 %copy-start = (f32[32,256]{1,0:T(8,128)S(1)}, f32[32,256]{1,0:T(8,128)}, u32[]{:S(2)}) copy-start(f32[32,256]{1,0:T(8,128)} %param.6) | copy-start | bytes 98308
  0.6 9.6 %copy-start.1 = (f32[32,2048]{1,0:T(8,128)S(1)}, f32[32,2048]{1,0:T(8,128)}, u32[]{:S(2)}) copy-start(f32[32,2048]{1,0:T(8,128)} %own.1) | copy-start | bytes 786436
  0.7 9.5 %collective-permute-start = (f32[32,2048]{1,0:T(8,128)}, f32[32,2048]{1,0:T(8,128)S(1)}, u32[]{:S(2)}, u32[]{:S(2)}) collective-permute-start(f32[32,2048]{1,0:T(8,128)} %own.1), channel_id=1, source_target_pairs={{0,16},{16,0},{1,17},{17,1},{2,18},{18,2},{3,19},{19,3},{4,20},{20... | collective-permute-start | bytes 786440 | tf_op jit(solution)/shard_map/ppermute | solution.py:497
  9.8 3.0 %collective-permute-start.2 = (bf16[16,128,128]{2,1,0:T(8,128)(2,1)S(1)}, bf16[16,128,128]{2,1,0:T(8,128)(2,1)S(1)}, u32[]{:S(2)}, u32[]{:S(2)}) collective-permute-start(bf16[16,128,128]{2,1,0:T(8,128)(2,1)S(1)} %get-tuple-element.17.give), channel_id=1, source_target_pairs={{0,1},{1,0},{2,3},{3,2},{4,5},{5,4},{6,7},{7,6},{8,9},{9,8},{10,11... | collective-permute-start | bytes 1572872 | tf_op jit(solution)/shard_map/ppermute | solution.py:501
  11.6 1.2 %collective-permute-start.1 = (f32[32,128]{1,0:T(8,128)S(1)}, f32[32,128]{1,0:T(8,128)S(1)}, u32[]{:S(2)}, u32[]{:S(2)}) collective-permute-start(f32[32,128]{1,0:T(8,128)S(1)} %get-tuple-element.18.acts), channel_id=1, source_target_pairs={{0,1},{1,0},{2,3},{3,2},{4,5},{5,4},{6,7},{7,6},{8,9},{9,8},{10,11... | collective-permute-start | bytes 49160 | tf_op jit(solution)/shard_map/ppermute | solution.py:523
  40.7 1.2 %collective-permute-start.3 = (f32[72,128]{1,0:T(8,128)S(1)}, f32[72,128]{1,0:T(8,128)S(1)}, u32[]{:S(2)}, u32[]{:S(2)}) collective-permute-start(f32[72,128]{1,0:T(8,128)S(1)} %partial.1.half), channel_id=1, source_target_pairs={{0,1},{1,0},{2,3},{3,2},{4,5},{5,4},{6,7},{7,6},{8,9},{9,8},{10,11... | collective-permute-start | bytes 110600 | tf_op jit(solution)/shard_map/ppermute | solution.py:530
  53.7 5.2 %collective-permute-start.4 = (f32[32,128]{1,0:T(8,128)S(1)}, f32[32,128]{1,0:T(8,128)S(1)}, u32[]{:S(2)}, u32[]{:S(2)}) collective-permute-start(f32[32,128]{1,0:T(8,128)S(1)} %get-tuple-element.29), channel_id=1, source_target_pairs={{0,16},{16,0},{1,17},{17,1},{2,18},{18,2},{3,19},{19,3},{4,20},{20... | collective-permute-start | bytes 49160 | tf_op jit(solution)/shard_map/ppermute | solution.py:537
  56.0 11.1 %all-to-all-start.3 = ((f16[32,16,128]{2,1,0:T(8,128)(2,1)}), f16[32,16,128]{2,1,0:T(8,128)(2,1)S(1)}, u32[]{:S(2)}, u32[]{:S(2)}) async-start(f16[32,16,128]{2,1,0:T(8,128)(2,1)} %bitcast.3), calls=%async_computation.3 | async-start | bytes 262144 | tf_op jit(solution)/shard_map/all_to_all | solution.py:507

commit v4 on v3

--- a/solution.py
+++ b/solution.py
@@ -533,11 +533,12 @@
             again_kernel, outs, "again", half, other_half, acts, sibling, keep, taken
         )
     got = exchange(parts)
-    acts, got = lax.optimization_barrier((acts, got))
-    partner = lax.ppermute(acts, "freq", swap)
     final, exps = local(last_kernel, [((2, OUTER // 4, LANES), f32), lane_rows], "last", got, mine)
     final = jnp.broadcast_to(final[:, None], (2, HALF // 2) + final.shape[1:])
-    got = exchange(final.reshape((HALF,) + final.shape[2:]), ("freq", "chips", "core"))
+    final = final.reshape((HALF,) + final.shape[2:]).astype(f16)
+    acts, final = lax.optimization_barrier((acts, final))
+    partner = lax.ppermute(acts, "freq", swap)
+    got = exchange(final, ("freq", "chips", "core"))
     components = local(
         natural_kernel,
         (w_start.shape, f32),

time: 68.5 us -> 68.4 us (level)
  transfers between devices with their start and end apart: 6 -> 6, of which waited for: 4 -> 4; matrix products, arithmetic and copies ran while one was open for 2% -> 1% of each run, Pallas kernels for 12% -> 11%
where the time goes in v4:
time: 68.4 us; the launch traced here: 68.1 us
  blocking collectives  37 us (54%)
  Pallas kernels  11.6 us (17%)
  waiting for transfers between devices  9.85 us (14%)
  starting transfers between devices  7.26 us (11%)
  other arithmetic  0.85 us (1%)
  between operations  0.79 us (1%)
  local copies, waits for them, and re-layouts  0.72 us (1%)
    all_to_all x3, blocking collectives, exchange(): lax.all_to_all(value.astype(f16), axes, split_axis=0, concat_axis=0, tile...  37 us
    all_to_all x1, waiting for transfers between devices, exchange(): lax.all_to_all(value.astype(f16), axes, split_axis=0, concat_axis=0, tile...  7.58 us
    pallas_call x1, Pallas kernels, spectrum(): pl.pallas_call(spectrum_kernel, out_shape=[jax.ShapeDtypeStruct((HALF //...  6.15 us
    pallas_call x7, Pallas kernels, local(): pl.pallas_call(kernel, out_shape=shapes if many else shapes[0], in_specs=...  5.48 us
    ppermute x1, starting transfers between devices, row_shards(): other = lax.ppermute(w_start, 'freq', swap)  3.03 us
    all_to_all x1, starting transfers between devices, exchange(): lax.all_to_all(value.astype(f16), axes, split_axis=0, concat_axis=0, tile...  2.88 us
  transfers between devices with their start and end apart: 6, of which 4 were waited for; matrix products, arithmetic and copies ran while one was open for 1% of the time, Pallas kernels for 11%

profile of v4, /device:TPU:0, one launch (start us, length us, event | category | flops | bytes accessed | tf_op | source)
XLA Modules:
  0.0 68.1 jit_solution(16035067869752031284)
XLA Ops:
  0.6 0.0 copy-start
  0.6 0.0 copy-start.1
  0.7 3.0 %collective-permute-start = (f32[32,2048]{1,0:T(8,128)}, f32[32,2048]{1,0:T(8,128)S(1)}, u32[]{:S(2)}, u32[]{:S(2)}) collective-permute-start(f32[32,2048]{1,0:T(8,128)} %own.1), channel_id=1, source_target_pairs={{0,16},{16,0},{1,17},{17,1},{2,18},{18,2},{3,19},{19,3},{4,20},{20... | collective-permute-start | bytes 786440 | tf_op jit(solution)/shard_map/ppermute | solution.py:497
  3.7 6.1 %spectrum.1 = (bf16[16,128,128]{2,1,0:T(8,128)(2,1)S(1)}, bf16[16,128,128]{2,1,0:T(8,128)(2,1)S(1)}, bf16[16,128]{1,0:T(8,128)(2,1)S(1)}) custom-call(s32[1]{0:T(128)} %bitcast.1.core, bf16[1,1048576]{1,0:T(2,128)(2,1)} %audio.1, f32[1216,128]{1,0:T(8,128)} %constant.24.clone.source), custom_call_target="tpu_custom_call" | custom-call | flops 2013265920 | bytes 4194304 | tf_op jit(solution)/shard_map/spectrum/pallas_call | solution.py:151
  9.8 0.1 collective-permute-start.2
  9.9 0.1 pad_add_fusion.at
  10.0 0.0 copy-done
  10.0 0.2 collective-permute-done.other
  10.2 0.0 copy-done.1
  10.2 1.4 %start.1 = (f32[32,128]{1,0:T(8,128)S(1)}, f32[32,128]{1,0:T(8,128)S(1)}) custom-call(s32[3]{0:T(128)S(1)} %pad_add_fusion.at, f32[32,2048]{1,0:T(8,128)S(1)} %copy-done.1, f32[32,2048]{1,0:T(8,128)S(1)} %collective-permute-done.other, bf16[16,128,128]{2,1,0:T(8,128)(2,1)S(1)} %get-tuple-element.16.keep, bf16[16,128,128]{2,1,0:T(8,128)(2,1)S(1)} %get-tuple-element.17.give, ...), custom_call_target="tpu_custom_call" | custom-call | flops 17179869184 | bytes 33554432 | tf_op jit(solution)/shard_map/start/pallas_call | solution.py:478
  11.6 0.4 collective-permute-start.1
  12.0 0.9 %collective-permute-done.1.sibling = f32[32,128]{1,0:T(8,128)S(1)} collective-permute-done((f32[32,128]{1,0:T(8,128)S(1)}, f32[32,128]{1,0:T(8,128)S(1)}, u32[]{:S(2)}, u32[]{:S(2)}) %collective-permute-start.1) | collective-permute-done | bytes 16416 | tf_op jit(solution)/shard_map/ppermute | solution.py:523
  12.8 0.0 collective-permute-done.2.taken
  12.9 0.5 sums.1
  13.4 15.1 %all_to_all.20 = f16[16,40,128]{2,1,0:T(8,128)(2,1)S(1)} all-to-all(f16[16,40,128]{2,1,0:T(8,128)(2,1)S(1)} %convert_element_type.29), channel_id=1, replica_groups=mesh['freq'=2,'chips'=8,'core'=2] {'freq','chips'}, dimensions={0} | all-to-all | bytes 327680 | tf_op jit(solution)/shard_map/all_to_all | solution.py:507
  28.5 0.5 slice.1
  29.0 11.0 %all_to_all.21 = f16[16,32,128]{2,1,0:T(8,128)(2,1)S(1)} all-to-all(f16[16,32,128]{2,1,0:T(8,128)(2,1)S(1)} %broadcast_in_dim.4), channel_id=1, replica_groups=mesh['freq'=2,'chips'=8,'core'=2] {'freq','chips'}, dimensions={0} | all-to-all | bytes 262144 | tf_op jit(solution)/shard_map/all_to_all | solution.py:507
  40.0 0.7 %partial.1.half = f32[72,128]{1,0:T(8,128)S(1)} custom-call(f32[16,32,128]{2,1,0:T(8,128)S(1)} %convert_element_type.32.got, f32[32,128]{1,0:T(8,128)S(1)} %get-tuple-element.21.exps, bf16[16,128,128]{2,1,0:T(8,128)(2,1)S(1)} %get-tuple-element.16.keep, bf16[16,128,128]{2,1,0:T(8,128)(2,1)S(1)} %collective-permute-done.2.taken, ...), custom_call_target="tpu_custom_call" | custom-call | tf_op jit(solution)/shard_map/partial/pallas_call | solution.py:478
  40.7 0.0 collective-permute-start.3
  40.8 1.2 %collective-permute-done.3.other_half = f32[72,128]{1,0:T(8,128)S(1)} collective-permute-done((f32[72,128]{1,0:T(8,128)S(1)}, f32[72,128]{1,0:T(8,128)S(1)}, u32[]{:S(2)}, u32[]{:S(2)}) %collective-permute-start.3) | collective-permute-done | bytes 36896 | tf_op jit(solution)/shard_map/ppermute | solution.py:530
  42.0 0.6 again.1
  42.6 11.0 %all_to_all.22 = f16[16,40,128]{2,1,0:T(8,128)(2,1)S(1)} all-to-all(f16[16,40,128]{2,1,0:T(8,128)(2,1)S(1)} %convert_element_type.33), channel_id=1, replica_groups=mesh['freq'=2,'chips'=8,'core'=2] {'freq','chips'}, dimensions={0} | all-to-all | bytes 327680 | tf_op jit(solution)/shard_map/all_to_all | solution.py:507
  53.7 0.7 last.1
  54.4 0.7 broadcast_in_dim.10
  55.1 0.9 %collective-permute-start.4 = (f32[32,128]{1,0:T(8,128)S(1)}, f32[32,128]{1,0:T(8,128)S(1)}, u32[]{:S(2)}, u32[]{:S(2)}) collective-permute-start(f32[32,128]{1,0:T(8,128)S(1)} %get-tuple-element.29), channel_id=1, source_target_pairs={{0,16},{16,0},{1,17},{17,1},{2,18},{18,2},{3,19},{19,3},{4,20},{20... | collective-permute-start | bytes 49160 | tf_op jit(solution)/shard_map/ppermute | solution.py:540
  56.0 2.9 %all-to-all-start.3 = ((f16[32,16,128]{2,1,0:T(8,128)(2,1)}), f16[32,16,128]{2,1,0:T(8,128)(2,1)S(1)}, u32[]{:S(2)}, u32[]{:S(2)}) async-start(f16[32,16,128]{2,1,0:T(8,128)(2,1)} %bitcast.3), calls=%async_computation.3 | async-start | bytes 262144 | tf_op jit(solution)/shard_map/all_to_all | solution.py:507
  58.9 0.0 collective-permute-done.4
  58.9 0.6 pad_maximum_fusion
  59.5 7.6 %all-to-all-done.3 = f16[32,16,128]{2,1,0:T(8,128)(2,1)S(1)} async-done(((f16[32,16,128]{2,1,0:T(8,128)(2,1)}), f16[32,16,128]{2,1,0:T(8,128)(2,1)S(1)}, u32[]{:S(2)}, u32[]{:S(2)}) %all-to-all-start.3) | async-done | bytes 131104 | tf_op jit(solution)/shard_map/all_to_all | solution.py:507
  67.1 1.0 %natural.1 = f32[32,2048]{1,0:T(8,128)} custom-call(f32[32,16,128]{2,1,0:T(8,128)S(1)} %convert_element_type.37.got, f32[32,128]{1,0:T(8,128)S(1)} %get-tuple-element.28.exps), custom_call_target="tpu_custom_call" | custom-call | tf_op jit(solution)/shard_map/natural/pallas_call | solution.py:478
  (11 shorter events, 0.2 us)
Async XLA Ops:
  0.6 9.4 %copy-start = (f32[32,256]{1,0:T(8,128)S(1)}, f32[32,256]{1,0:T(8,128)}, u32[]{:S(2)}) copy-start(f32[32,256]{1,0:T(8,128)} %param.6) | copy-start | bytes 98308
  0.6 9.6 %copy-start.1 = (f32[32,2048]{1,0:T(8,128)S(1)}, f32[32,2048]{1,0:T(8,128)}, u32[]{:S(2)}) copy-start(f32[32,2048]{1,0:T(8,128)} %own.1) | copy-start | bytes 786436
  0.7 9.5 %collective-permute-start = (f32[32,2048]{1,0:T(8,128)}, f32[32,2048]{1,0:T(8,128)S(1)}, u32[]{:S(2)}, u32[]{:S(2)}) collective-permute-start(f32[32,2048]{1,0:T(8,128)} %own.1), channel_id=1, source_target_pairs={{0,16},{16,0},{1,17},{17,1},{2,18},{18,2},{3,19},{19,3},{4,20},{20... | collective-permute-start | bytes 786440 | tf_op jit(solution)/shard_map/ppermute | solution.py:497
  9.8 3.0 %collective-permute-start.2 = (bf16[16,128,128]{2,1,0:T(8,128)(2,1)S(1)}, bf16[16,128,128]{2,1,0:T(8,128)(2,1)S(1)}, u32[]{:S(2)}, u32[]{:S(2)}) collective-permute-start(bf16[16,128,128]{2,1,0:T(8,128)(2,1)S(1)} %get-tuple-element.17.give), channel_id=1, source_target_pairs={{0,1},{1,0},{2,3},{3,2},{4,5},{5,4},{6,7},{7,6},{8,9},{9,8},{10,11... | collective-permute-start | bytes 1572872 | tf_op jit(solution)/shard_map/ppermute | solution.py:501
  11.6 1.2 %collective-permute-start.1 = (f32[32,128]{1,0:T(8,128)S(1)}, f32[32,128]{1,0:T(8,128)S(1)}, u32[]{:S(2)}, u32[]{:S(2)}) collective-permute-start(f32[32,128]{1,0:T(8,128)S(1)} %get-tuple-element.18.acts), channel_id=1, source_target_pairs={{0,1},{1,0},{2,3},{3,2},{4,5},{5,4},{6,7},{7,6},{8,9},{9,8},{10,11... | collective-permute-start | bytes 49160 | tf_op jit(solution)/shard_map/ppermute | solution.py:523
  40.7 1.2 %collective-permute-start.3 = (f32[72,128]{1,0:T(8,128)S(1)}, f32[72,128]{1,0:T(8,128)S(1)}, u32[]{:S(2)}, u32[]{:S(2)}) collective-permute-start(f32[72,128]{1,0:T(8,128)S(1)} %partial.1.half), channel_id=1, source_target_pairs={{0,1},{1,0},{2,3},{3,2},{4,5},{5,4},{6,7},{7,6},{8,9},{9,8},{10,11... | collective-permute-start | bytes 110600 | tf_op jit(solution)/shard_map/ppermute | solution.py:530
  55.1 3.8 %collective-permute-start.4 = (f32[32,128]{1,0:T(8,128)S(1)}, f32[32,128]{1,0:T(8,128)S(1)}, u32[]{:S(2)}, u32[]{:S(2)}) collective-permute-start(f32[32,128]{1,0:T(8,128)S(1)} %get-tuple-element.29), channel_id=1, source_target_pairs={{0,16},{16,0},{1,17},{17,1},{2,18},{18,2},{3,19},{19,3},{4,20},{20... | collective-permute-start | bytes 49160 | tf_op jit(solution)/shard_map/ppermute | solution.py:540
  56.0 11.1 %all-to-all-start.3 = ((f16[32,16,128]{2,1,0:T(8,128)(2,1)}), f16[32,16,128]{2,1,0:T(8,128)(2,1)S(1)}, u32[]{:S(2)}, u32[]{:S(2)}) async-start(f16[32,16,128]{2,1,0:T(8,128)(2,1)} %bitcast.3), calls=%async_computation.3 | async-start | bytes 262144 | tf_op jit(solution)/shard_map/all_to_all | solution.py:507

commit v5 on v2

--- a/solution.py
+++ b/solution.py
@@ -317,7 +317,7 @@
         axis=1,
     )
     total = jnp.zeros((acts.shape[1], LANES), jnp.float32)
-    batch = 8
+    batch = SIDE
     for grid, start in ((keep, side * SIDE), (give, (1 - side) * SIDE)):
         for base in range(0, SIDE, batch):
             pieces = []

time: 67.8 us -> 67.8 us (level)
  no operation moved by 1% of the time
where the time goes in v5:
time: 67.8 us; the launch traced here: 67.5 us
  blocking collectives  37 us (55%)
  Pallas kernels  12.2 us (18%)
  waiting for transfers between devices  8.77 us (13%)
  starting transfers between devices  7.78 us (11%)
  between operations  0.78 us (1%)
  local copies, waits for them, and re-layouts  0.72 us (1%)
    all_to_all x3, blocking collectives, exchange(): lax.all_to_all(value.astype(f16), axes, split_axis=0, concat_axis=0, tile...  37 us
    all_to_all x1, waiting for transfers between devices, exchange(): lax.all_to_all(value.astype(f16), axes, split_axis=0, concat_axis=0, tile...  6.51 us
    pallas_call x1, Pallas kernels, spectrum(): pl.pallas_call(spectrum_kernel, out_shape=[jax.ShapeDtypeStruct((HALF //...  6.15 us
    pallas_call x7, Pallas kernels, local(): pl.pallas_call(kernel, out_shape=shapes if many else shapes[0], in_specs=...  6.02 us
    ppermute x1, starting transfers between devices, row_shards(): other = lax.ppermute(w_start, 'freq', swap)  3.03 us
    all_to_all x1, starting transfers between devices, exchange(): lax.all_to_all(value.astype(f16), axes, split_axis=0, concat_axis=0, tile...  2.58 us
    ppermute x1, starting transfers between devices, row_shards(): partner = lax.ppermute(acts, 'freq', swap)  1.72 us
  transfers between devices with their start and end apart: 6, of which 4 were waited for; matrix products, arithmetic and copies ran while one was open for 0% of the time, Pallas kernels for 11%

profile of v5, /device:TPU:0, one launch (start us, length us, event | category | flops | bytes accessed | tf_op | source)
XLA Modules:
  0.0 67.5 jit_solution(13162193560046337394)
XLA Ops:
  0.6 0.0 copy-start
  0.6 0.0 copy-start.1
  0.7 3.0 %collective-permute-start = (f32[32,2048]{1,0:T(8,128)}, f32[32,2048]{1,0:T(8,128)S(1)}, u32[]{:S(2)}, u32[]{:S(2)}) collective-permute-start(f32[32,2048]{1,0:T(8,128)} %own.1), channel_id=1, source_target_pairs={{0,16},{16,0},{1,17},{17,1},{2,18},{18,2},{3,19},{19,3},{4,20},{20... | collective-permute-start | bytes 786440 | tf_op jit(solution)/shard_map/ppermute | solution.py:499
  3.7 6.1 %spectrum.1 = (bf16[16,128,128]{2,1,0:T(8,128)(2,1)S(1)}, bf16[16,128,128]{2,1,0:T(8,128)(2,1)S(1)}, bf16[16,128]{1,0:T(8,128)(2,1)S(1)}) custom-call(s32[1]{0:T(128)} %bitcast.1.core, bf16[1,1048576]{1,0:T(2,128)(2,1)} %audio.1, f32[1216,128]{1,0:T(8,128)} %constant.24.clone.source), custom_call_target="tpu_custom_call" | custom-call | flops 2013265920 | bytes 4194304 | tf_op jit(solution)/shard_map/spectrum/pallas_call | solution.py:151
  9.8 0.1 collective-permute-start.2
  9.9 0.1 pad_add_fusion.at
  10.0 0.0 copy-done
  10.0 0.2 collective-permute-done.other
  10.2 0.0 copy-done.1
  10.2 1.4 %start.1 = (f32[32,128]{1,0:T(8,128)S(1)}, f32[32,128]{1,0:T(8,128)S(1)}) custom-call(s32[3]{0:T(128)S(1)} %pad_add_fusion.at, f32[32,2048]{1,0:T(8,128)S(1)} %copy-done.1, f32[32,2048]{1,0:T(8,128)S(1)} %collective-permute-done.other, bf16[16,128,128]{2,1,0:T(8,128)(2,1)S(1)} %get-tuple-element.16.keep, bf16[16,128,128]{2,1,0:T(8,128)(2,1)S(1)} %get-tuple-element.17.give, ...), custom_call_target="tpu_custom_call" | custom-call | flops 17179869184 | bytes 33554432 | tf_op jit(solution)/shard_map/start/pallas_call | solution.py:480
  11.6 0.4 collective-permute-start.1
  12.0 0.9 %collective-permute-done.1.sibling = f32[32,128]{1,0:T(8,128)S(1)} collective-permute-done((f32[32,128]{1,0:T(8,128)S(1)}, f32[32,128]{1,0:T(8,128)S(1)}, u32[]{:S(2)}, u32[]{:S(2)}) %collective-permute-start.1) | collective-permute-done | bytes 16416 | tf_op jit(solution)/shard_map/ppermute | solution.py:525
  12.8 0.0 collective-permute-done.2.taken
  12.9 0.5 sums.1
  13.4 15.1 %all_to_all.20 = f16[16,40,128]{2,1,0:T(8,128)(2,1)S(1)} all-to-all(f16[16,40,128]{2,1,0:T(8,128)(2,1)S(1)} %convert_element_type.29), channel_id=1, replica_groups=mesh['freq'=2,'chips'=8,'core'=2] {'freq','chips'}, dimensions={0} | all-to-all | bytes 327680 | tf_op jit(solution)/shard_map/all_to_all | solution.py:509
  28.5 0.5 slice.1
  29.0 11.0 %all_to_all.21 = f16[16,32,128]{2,1,0:T(8,128)(2,1)S(1)} all-to-all(f16[16,32,128]{2,1,0:T(8,128)(2,1)S(1)} %broadcast_in_dim.4), channel_id=1, replica_groups=mesh['freq'=2,'chips'=8,'core'=2] {'freq','chips'}, dimensions={0} | all-to-all | bytes 262144 | tf_op jit(solution)/shard_map/all_to_all | solution.py:509
  40.0 0.7 %partial.1.half = f32[72,128]{1,0:T(8,128)S(1)} custom-call(f32[16,32,128]{2,1,0:T(8,128)S(1)} %convert_element_type.32.got, f32[32,128]{1,0:T(8,128)S(1)} %get-tuple-element.21.exps, bf16[16,128,128]{2,1,0:T(8,128)(2,1)S(1)} %get-tuple-element.16.keep, bf16[16,128,128]{2,1,0:T(8,128)(2,1)S(1)} %collective-permute-done.2.taken, ...), custom_call_target="tpu_custom_call" | custom-call | tf_op jit(solution)/shard_map/partial/pallas_call | solution.py:480
  40.7 0.0 collective-permute-start.3
  40.8 1.2 %collective-permute-done.3.other_half = f32[72,128]{1,0:T(8,128)S(1)} collective-permute-done((f32[72,128]{1,0:T(8,128)S(1)}, f32[72,128]{1,0:T(8,128)S(1)}, u32[]{:S(2)}, u32[]{:S(2)}) %collective-permute-start.3) | collective-permute-done | bytes 36896 | tf_op jit(solution)/shard_map/ppermute | solution.py:532
  42.0 0.6 again.1
  42.6 11.0 %all_to_all.22 = f16[16,40,128]{2,1,0:T(8,128)(2,1)S(1)} all-to-all(f16[16,40,128]{2,1,0:T(8,128)(2,1)S(1)} %convert_element_type.33), channel_id=1, replica_groups=mesh['freq'=2,'chips'=8,'core'=2] {'freq','chips'}, dimensions={0} | all-to-all | bytes 327680 | tf_op jit(solution)/shard_map/all_to_all | solution.py:509
  53.7 0.7 last.1
  54.4 0.7 %broadcast_in_dim.10 = f16[2,16,16,128]{3,2,1,0:T(8,128)(2,1)} broadcast(f16[2,16,128]{2,1,0:T(8,128)(2,1)S(1)} %convert_element_type.35), dimensions={0,2,3} | broadcast | bytes 139264 | tf_op jit(solution)/shard_map/broadcast_in_dim | solution.py:541
  55.1 2.6 %all-to-all-start.3 = ((f16[32,16,128]{2,1,0:T(8,128)(2,1)}), f16[32,16,128]{2,1,0:T(8,128)(2,1)S(1)}, u32[]{:S(2)}, u32[]{:S(2)}) async-start(f16[32,16,128]{2,1,0:T(8,128)(2,1)} %bitcast.3), calls=%async_computation.3 | async-start | bytes 262144 | tf_op jit(solution)/shard_map/all_to_all | solution.py:509
  57.7 1.7 %collective-permute-start.4 = (f32[32,128]{1,0:T(8,128)S(1)}, f32[32,128]{1,0:T(8,128)S(1)}, u32[]{:S(2)}, u32[]{:S(2)}) collective-permute-start(f32[32,128]{1,0:T(8,128)S(1)} %get-tuple-element.29.acts), channel_id=1, source_target_pairs={{0,16},{16,0},{1,17},{17,1},{2,18},{18,2},{3,19},{19,3},{4,20},{20... | collective-permute-start | bytes 49160 | tf_op jit(solution)/shard_map/ppermute | solution.py:539
  59.4 6.5 %all-to-all-done.3 = f16[32,16,128]{2,1,0:T(8,128)(2,1)S(1)} async-done(((f16[32,16,128]{2,1,0:T(8,128)(2,1)}), f16[32,16,128]{2,1,0:T(8,128)(2,1)S(1)}, u32[]{:S(2)}, u32[]{:S(2)}) %all-to-all-start.3) | async-done | bytes 131104 | tf_op jit(solution)/shard_map/all_to_all | solution.py:509
  65.9 0.0 collective-permute-done.4.partner
  65.9 1.6 %natural.1 = (f32[32,2048]{1,0:T(8,128)}, f32[32,256]{1,0:T(8,128)}) custom-call(s32[3]{0:T(128)S(1)} %pad_add_fusion.at, f32[32,16,128]{2,1,0:T(8,128)S(1)} %convert_element_type.37.got, f32[32,128]{1,0:T(8,128)S(1)} %get-tuple-element.28.exps, f32[32,128]{1,0:T(8,128)S(1)} %get-tuple-element.29.acts, f32[32,128]{1,0:T(8,128)S(1)} %collective-permute-done.4.partner), custom_call_target="tpu_custom_call" | custom-call | tf_op jit(solution)/shard_map/natural/pallas_call | solution.py:480
  (10 shorter events, 0.2 us)
Async XLA Ops:
  0.6 9.4 %copy-start = (f32[32,256]{1,0:T(8,128)S(1)}, f32[32,256]{1,0:T(8,128)}, u32[]{:S(2)}) copy-start(f32[32,256]{1,0:T(8,128)} %param.6) | copy-start | bytes 98308
  0.6 9.6 %copy-start.1 = (f32[32,2048]{1,0:T(8,128)S(1)}, f32[32,2048]{1,0:T(8,128)}, u32[]{:S(2)}) copy-start(f32[32,2048]{1,0:T(8,128)} %own.1) | copy-start | bytes 786436
  0.7 9.5 %collective-permute-start = (f32[32,2048]{1,0:T(8,128)}, f32[32,2048]{1,0:T(8,128)S(1)}, u32[]{:S(2)}, u32[]{:S(2)}) collective-permute-start(f32[32,2048]{1,0:T(8,128)} %own.1), channel_id=1, source_target_pairs={{0,16},{16,0},{1,17},{17,1},{2,18},{18,2},{3,19},{19,3},{4,20},{20... | collective-permute-start | bytes 786440 | tf_op jit(solution)/shard_map/ppermute | solution.py:499
  9.8 3.0 %collective-permute-start.2 = (bf16[16,128,128]{2,1,0:T(8,128)(2,1)S(1)}, bf16[16,128,128]{2,1,0:T(8,128)(2,1)S(1)}, u32[]{:S(2)}, u32[]{:S(2)}) collective-permute-start(bf16[16,128,128]{2,1,0:T(8,128)(2,1)S(1)} %get-tuple-element.17.give), channel_id=1, source_target_pairs={{0,1},{1,0},{2,3},{3,2},{4,5},{5,4},{6,7},{7,6},{8,9},{9,8},{10,11... | collective-permute-start | bytes 1572872 | tf_op jit(solution)/shard_map/ppermute | solution.py:503
  11.6 1.2 %collective-permute-start.1 = (f32[32,128]{1,0:T(8,128)S(1)}, f32[32,128]{1,0:T(8,128)S(1)}, u32[]{:S(2)}, u32[]{:S(2)}) collective-permute-start(f32[32,128]{1,0:T(8,128)S(1)} %get-tuple-element.18.acts), channel_id=1, source_target_pairs={{0,1},{1,0},{2,3},{3,2},{4,5},{5,4},{6,7},{7,6},{8,9},{9,8},{10,11... | collective-permute-start | bytes 49160 | tf_op jit(solution)/shard_map/ppermute | solution.py:525
  40.7 1.2 %collective-permute-start.3 = (f32[72,128]{1,0:T(8,128)S(1)}, f32[72,128]{1,0:T(8,128)S(1)}, u32[]{:S(2)}, u32[]{:S(2)}) collective-permute-start(f32[72,128]{1,0:T(8,128)S(1)} %partial.1.half), channel_id=1, source_target_pairs={{0,1},{1,0},{2,3},{3,2},{4,5},{5,4},{6,7},{7,6},{8,9},{9,8},{10,11... | collective-permute-start | bytes 110600 | tf_op jit(solution)/shard_map/ppermute | solution.py:532
  55.1 10.8 %all-to-all-start.3 = ((f16[32,16,128]{2,1,0:T(8,128)(2,1)}), f16[32,16,128]{2,1,0:T(8,128)(2,1)S(1)}, u32[]{:S(2)}, u32[]{:S(2)}) async-start(f16[32,16,128]{2,1,0:T(8,128)(2,1)} %bitcast.3), calls=%async_computation.3 | async-start | bytes 262144 | tf_op jit(solution)/shard_map/all_to_all | solution.py:509
  57.7 8.3 %collective-permute-start.4 = (f32[32,128]{1,0:T(8,128)S(1)}, f32[32,128]{1,0:T(8,128)S(1)}, u32[]{:S(2)}, u32[]{:S(2)}) collective-permute-start(f32[32,128]{1,0:T(8,128)S(1)} %get-tuple-element.29.acts), channel_id=1, source_target_pairs={{0,16},{16,0},{1,17},{17,1},{2,18},{18,2},{3,19},{19,3},{4,20},{20... | collective-permute-start | bytes 49160 | tf_op jit(solution)/shard_map/ppermute | solution.py:539

commit v6 on v5

--- a/solution.py
+++ b/solution.py
@@ -534,9 +534,8 @@
         parts, acts = local(
             again_kernel, outs, "again", half, other_half, acts, sibling, keep, taken
         )
+    partner = lax.ppermute(acts, "freq", swap)
     got = exchange(parts)
-    acts, got = lax.optimization_barrier((acts, got))
-    partner = lax.ppermute(acts, "freq", swap)
     final, exps = local(last_kernel, [((2, OUTER // 4, LANES), f32), lane_rows], "last", got, mine)
     final = jnp.broadcast_to(final[:, None], (2, HALF // 2) + final.shape[1:])
     got = exchange(final.reshape((HALF,) + final.shape[2:]), ("freq", "chips", "core"))

time: 67.8 us -> 67.8 us (level)
  no operation moved by 1% of the time
where the time goes in v6:
time: 67.8 us; the launch traced here: 67.5 us
  blocking collectives  37 us (55%)
  Pallas kernels  12.2 us (18%)
  waiting for transfers between devices  8.77 us (13%)
  starting transfers between devices  7.78 us (11%)
  between operations  0.78 us (1%)
  local copies, waits for them, and re-layouts  0.72 us (1%)
    all_to_all x3, blocking collectives, exchange(): lax.all_to_all(value.astype(f16), axes, split_axis=0, concat_axis=0, tile...  37 us
    all_to_all x1, waiting for transfers between devices, exchange(): lax.all_to_all(value.astype(f16), axes, split_axis=0, concat_axis=0, tile...  6.51 us
    pallas_call x1, Pallas kernels, spectrum(): pl.pallas_call(spectrum_kernel, out_shape=[jax.ShapeDtypeStruct((HALF //...  6.15 us
    pallas_call x7, Pallas kernels, local(): pl.pallas_call(kernel, out_shape=shapes if many else shapes[0], in_specs=...  6.02 us
    ppermute x1, starting transfers between devices, row_shards(): other = lax.ppermute(w_start, 'freq', swap)  3.03 us
    all_to_all x1, starting transfers between devices, exchange(): lax.all_to_all(value.astype(f16), axes, split_axis=0, concat_axis=0, tile...  2.58 us
    ppermute x1, starting transfers between devices, row_shards(): partner = lax.ppermute(acts, 'freq', swap)  1.72 us
  transfers between devices with their start and end apart: 6, of which 4 were waited for; matrix products, arithmetic and copies ran while one was open for 0% of the time, Pallas kernels for 11%

profile of v6, /device:TPU:0, one launch (start us, length us, event | category | flops | bytes accessed | tf_op | source)
XLA Modules:
  0.0 67.5 jit_solution(13162193560046337394)
XLA Ops:
  0.6 0.0 copy-start
  0.6 0.0 copy-start.1
  0.7 3.0 %collective-permute-start = (f32[32,2048]{1,0:T(8,128)}, f32[32,2048]{1,0:T(8,128)S(1)}, u32[]{:S(2)}, u32[]{:S(2)}) collective-permute-start(f32[32,2048]{1,0:T(8,128)} %own.1), channel_id=1, source_target_pairs={{0,16},{16,0},{1,17},{17,1},{2,18},{18,2},{3,19},{19,3},{4,20},{20... | collective-permute-start | bytes 786440 | tf_op jit(solution)/shard_map/ppermute | solution.py:499
  3.7 6.1 %spectrum.1 = (bf16[16,128,128]{2,1,0:T(8,128)(2,1)S(1)}, bf16[16,128,128]{2,1,0:T(8,128)(2,1)S(1)}, bf16[16,128]{1,0:T(8,128)(2,1)S(1)}) custom-call(s32[1]{0:T(128)} %bitcast.1.core, bf16[1,1048576]{1,0:T(2,128)(2,1)} %audio.1, f32[1216,128]{1,0:T(8,128)} %constant.24.clone.source), custom_call_target="tpu_custom_call" | custom-call | flops 2013265920 | bytes 4194304 | tf_op jit(solution)/shard_map/spectrum/pallas_call | solution.py:151
  9.8 0.1 collective-permute-start.2
  9.9 0.1 pad_add_fusion.at
  10.0 0.0 copy-done
  10.0 0.2 collective-permute-done.other
  10.2 0.0 copy-done.1
  10.2 1.4 %start.1 = (f32[32,128]{1,0:T(8,128)S(1)}, f32[32,128]{1,0:T(8,128)S(1)}) custom-call(s32[3]{0:T(128)S(1)} %pad_add_fusion.at, f32[32,2048]{1,0:T(8,128)S(1)} %copy-done.1, f32[32,2048]{1,0:T(8,128)S(1)} %collective-permute-done.other, bf16[16,128,128]{2,1,0:T(8,128)(2,1)S(1)} %get-tuple-element.14.keep, bf16[16,128,128]{2,1,0:T(8,128)(2,1)S(1)} %get-tuple-element.15.give, ...), custom_call_target="tpu_custom_call" | custom-call | flops 17179869184 | bytes 33554432 | tf_op jit(solution)/shard_map/start/pallas_call | solution.py:480
  11.6 0.4 collective-permute-start.1
  12.0 0.9 %collective-permute-done.1.sibling = f32[32,128]{1,0:T(8,128)S(1)} collective-permute-done((f32[32,128]{1,0:T(8,128)S(1)}, f32[32,128]{1,0:T(8,128)S(1)}, u32[]{:S(2)}, u32[]{:S(2)}) %collective-permute-start.1) | collective-permute-done | bytes 16416 | tf_op jit(solution)/shard_map/ppermute | solution.py:525
  12.8 0.0 collective-permute-done.2.taken
  12.9 0.5 sums.1
  13.4 15.1 %all_to_all.20 = f16[16,40,128]{2,1,0:T(8,128)(2,1)S(1)} all-to-all(f16[16,40,128]{2,1,0:T(8,128)(2,1)S(1)} %convert_element_type.29), channel_id=1, replica_groups=mesh['freq'=2,'chips'=8,'core'=2] {'freq','chips'}, dimensions={0} | all-to-all | bytes 327680 | tf_op jit(solution)/shard_map/all_to_all | solution.py:509
  28.5 0.5 slice.1
  29.0 11.0 %all_to_all.21 = f16[16,32,128]{2,1,0:T(8,128)(2,1)S(1)} all-to-all(f16[16,32,128]{2,1,0:T(8,128)(2,1)S(1)} %broadcast_in_dim.4), channel_id=1, replica_groups=mesh['freq'=2,'chips'=8,'core'=2] {'freq','chips'}, dimensions={0} | all-to-all | bytes 262144 | tf_op jit(solution)/shard_map/all_to_all | solution.py:509
  40.0 0.7 %partial.1.half = f32[72,128]{1,0:T(8,128)S(1)} custom-call(f32[16,32,128]{2,1,0:T(8,128)S(1)} %convert_element_type.32.got, f32[32,128]{1,0:T(8,128)S(1)} %get-tuple-element.19.exps, bf16[16,128,128]{2,1,0:T(8,128)(2,1)S(1)} %get-tuple-element.14.keep, bf16[16,128,128]{2,1,0:T(8,128)(2,1)S(1)} %collective-permute-done.2.taken, ...), custom_call_target="tpu_custom_call" | custom-call | tf_op jit(solution)/shard_map/partial/pallas_call | solution.py:480
  40.7 0.0 collective-permute-start.3
  40.8 1.2 %collective-permute-done.3.other_half = f32[72,128]{1,0:T(8,128)S(1)} collective-permute-done((f32[72,128]{1,0:T(8,128)S(1)}, f32[72,128]{1,0:T(8,128)S(1)}, u32[]{:S(2)}, u32[]{:S(2)}) %collective-permute-start.3) | collective-permute-done | bytes 36896 | tf_op jit(solution)/shard_map/ppermute | solution.py:532
  42.0 0.6 again.1
  42.6 11.0 %all_to_all.22 = f16[16,40,128]{2,1,0:T(8,128)(2,1)S(1)} all-to-all(f16[16,40,128]{2,1,0:T(8,128)(2,1)S(1)} %convert_element_type.33), channel_id=1, replica_groups=mesh['freq'=2,'chips'=8,'core'=2] {'freq','chips'}, dimensions={0} | all-to-all | bytes 327680 | tf_op jit(solution)/shard_map/all_to_all | solution.py:509
  53.7 0.7 last.1
  54.4 0.7 %broadcast_in_dim.10 = f16[2,16,16,128]{3,2,1,0:T(8,128)(2,1)} broadcast(f16[2,16,128]{2,1,0:T(8,128)(2,1)S(1)} %convert_element_type.35), dimensions={0,2,3} | broadcast | bytes 139264 | tf_op jit(solution)/shard_map/broadcast_in_dim | solution.py:540
  55.1 2.6 %all-to-all-start.3 = ((f16[32,16,128]{2,1,0:T(8,128)(2,1)}), f16[32,16,128]{2,1,0:T(8,128)(2,1)S(1)}, u32[]{:S(2)}, u32[]{:S(2)}) async-start(f16[32,16,128]{2,1,0:T(8,128)(2,1)} %bitcast.3), calls=%async_computation.3 | async-start | bytes 262144 | tf_op jit(solution)/shard_map/all_to_all | solution.py:509
  57.7 1.7 %collective-permute-start.4 = (f32[32,128]{1,0:T(8,128)S(1)}, f32[32,128]{1,0:T(8,128)S(1)}, u32[]{:S(2)}, u32[]{:S(2)}) collective-permute-start(f32[32,128]{1,0:T(8,128)S(1)} %get-tuple-element.25.acts), channel_id=1, source_target_pairs={{0,16},{16,0},{1,17},{17,1},{2,18},{18,2},{3,19},{19,3},{4,20},{20... | collective-permute-start | bytes 49160 | tf_op jit(solution)/shard_map/ppermute | solution.py:537
  59.4 6.5 %all-to-all-done.3 = f16[32,16,128]{2,1,0:T(8,128)(2,1)S(1)} async-done(((f16[32,16,128]{2,1,0:T(8,128)(2,1)}), f16[32,16,128]{2,1,0:T(8,128)(2,1)S(1)}, u32[]{:S(2)}, u32[]{:S(2)}) %all-to-all-start.3) | async-done | bytes 131104 | tf_op jit(solution)/shard_map/all_to_all | solution.py:509
  65.9 0.0 collective-permute-done.4.partner
  65.9 1.6 %natural.1 = (f32[32,2048]{1,0:T(8,128)}, f32[32,256]{1,0:T(8,128)}) custom-call(s32[3]{0:T(128)S(1)} %pad_add_fusion.at, f32[32,16,128]{2,1,0:T(8,128)S(1)} %convert_element_type.37.got, f32[32,128]{1,0:T(8,128)S(1)} %get-tuple-element.24.exps, f32[32,128]{1,0:T(8,128)S(1)} %get-tuple-element.25.acts, f32[32,128]{1,0:T(8,128)S(1)} %collective-permute-done.4.partner), custom_call_target="tpu_custom_call" | custom-call | tf_op jit(solution)/shard_map/natural/pallas_call | solution.py:480
  (10 shorter events, 0.2 us)
Async XLA Ops:
  0.6 9.4 %copy-start = (f32[32,256]{1,0:T(8,128)S(1)}, f32[32,256]{1,0:T(8,128)}, u32[]{:S(2)}) copy-start(f32[32,256]{1,0:T(8,128)} %param.6) | copy-start | bytes 98308
  0.6 9.6 %copy-start.1 = (f32[32,2048]{1,0:T(8,128)S(1)}, f32[32,2048]{1,0:T(8,128)}, u32[]{:S(2)}) copy-start(f32[32,2048]{1,0:T(8,128)} %own.1) | copy-start | bytes 786436
  0.7 9.5 %collective-permute-start = (f32[32,2048]{1,0:T(8,128)}, f32[32,2048]{1,0:T(8,128)S(1)}, u32[]{:S(2)}, u32[]{:S(2)}) collective-permute-start(f32[32,2048]{1,0:T(8,128)} %own.1), channel_id=1, source_target_pairs={{0,16},{16,0},{1,17},{17,1},{2,18},{18,2},{3,19},{19,3},{4,20},{20... | collective-permute-start | bytes 786440 | tf_op jit(solution)/shard_map/ppermute | solution.py:499
  9.8 3.0 %collective-permute-start.2 = (bf16[16,128,128]{2,1,0:T(8,128)(2,1)S(1)}, bf16[16,128,128]{2,1,0:T(8,128)(2,1)S(1)}, u32[]{:S(2)}, u32[]{:S(2)}) collective-permute-start(bf16[16,128,128]{2,1,0:T(8,128)(2,1)S(1)} %get-tuple-element.15.give), channel_id=1, source_target_pairs={{0,1},{1,0},{2,3},{3,2},{4,5},{5,4},{6,7},{7,6},{8,9},{9,8},{10,11... | collective-permute-start | bytes 1572872 | tf_op jit(solution)/shard_map/ppermute | solution.py:503
  11.6 1.2 %collective-permute-start.1 = (f32[32,128]{1,0:T(8,128)S(1)}, f32[32,128]{1,0:T(8,128)S(1)}, u32[]{:S(2)}, u32[]{:S(2)}) collective-permute-start(f32[32,128]{1,0:T(8,128)S(1)} %get-tuple-element.16.acts), channel_id=1, source_target_pairs={{0,1},{1,0},{2,3},{3,2},{4,5},{5,4},{6,7},{7,6},{8,9},{9,8},{10,11... | collective-permute-start | bytes 49160 | tf_op jit(solution)/shard_map/ppermute | solution.py:525
  40.7 1.2 %collective-permute-start.3 = (f32[72,128]{1,0:T(8,128)S(1)}, f32[72,128]{1,0:T(8,128)S(1)}, u32[]{:S(2)}, u32[]{:S(2)}) collective-permute-start(f32[72,128]{1,0:T(8,128)S(1)} %partial.1.half), channel_id=1, source_target_pairs={{0,1},{1,0},{2,3},{3,2},{4,5},{5,4},{6,7},{7,6},{8,9},{9,8},{10,11... | collective-permute-start | bytes 110600 | tf_op jit(solution)/shard_map/ppermute | solution.py:532
  55.1 10.8 %all-to-all-start.3 = ((f16[32,16,128]{2,1,0:T(8,128)(2,1)}), f16[32,16,128]{2,1,0:T(8,128)(2,1)S(1)}, u32[]{:S(2)}, u32[]{:S(2)}) async-start(f16[32,16,128]{2,1,0:T(8,128)(2,1)} %bitcast.3), calls=%async_computation.3 | async-start | bytes 262144 | tf_op jit(solution)/shard_map/all_to_all | solution.py:509
  57.7 8.3 %collective-permute-start.4 = (f32[32,128]{1,0:T(8,128)S(1)}, f32[32,128]{1,0:T(8,128)S(1)}, u32[]{:S(2)}, u32[]{:S(2)}) collective-permute-start(f32[32,128]{1,0:T(8,128)S(1)} %get-tuple-element.25.acts), channel_id=1, source_target_pairs={{0,16},{16,0},{1,17},{17,1},{2,18},{18,2},{3,19},{19,3},{4,20},{20... | collective-permute-start | bytes 49160 | tf_op jit(solution)/shard_map/ppermute | solution.py:537

commit v7 on v5

--- a/solution.py
+++ b/solution.py
@@ -302,6 +302,7 @@
     gram = gram_of(wide)
     span = OUTER // quads
     block = places((span, LANES))[1] // comp
+    masks = [jnp.where(block == c, 1.0, 0.0).astype(jnp.bfloat16) for c in range(quads)]
 
     def pair(r):
         mirror = jnp.where(r == 0, HALF, OUTER - r)
@@ -323,7 +324,8 @@
             pieces = []
             for u in range(base, base + batch):
                 for value in pair(start + u):
-                    pieces += [jnp.where(block == c, value, 0.0).astype(jnp.bfloat16) for c in range(quads)]
+                    short = value.astype(jnp.bfloat16)
+                    pieces += [short * mask for mask in masks]
             left = jnp.concatenate([grid[u] for u in range(base, base + batch)], axis=1)
             total += jnp.dot(left, jnp.concatenate(pieces, axis=0), preferred_element_type=jnp.float32)
     total = total.T

time: 67.8 us -> 67.8 us (level)
  no operation moved by 1% of the time
where the time goes in v7:
time: 67.8 us; the launch traced here: 67.5 us
  blocking collectives  37 us (55%)
  Pallas kernels  12.2 us (18%)
  waiting for transfers between devices  8.77 us (13%)
  starting transfers between devices  7.78 us (11%)
  between operations  0.78 us (1%)
  local copies, waits for them, and re-layouts  0.72 us (1%)
    all_to_all x3, blocking collectives, exchange(): lax.all_to_all(value.astype(f16), axes, split_axis=0, concat_axis=0, tile...  37 us
    all_to_all x1, waiting for transfers between devices, exchange(): lax.all_to_all(value.astype(f16), axes, split_axis=0, concat_axis=0, tile...  6.51 us
    pallas_call x1, Pallas kernels, spectrum(): pl.pallas_call(spectrum_kernel, out_shape=[jax.ShapeDtypeStruct((HALF //...  6.15 us
    pallas_call x7, Pallas kernels, local(): pl.pallas_call(kernel, out_shape=shapes if many else shapes[0], in_specs=...  6.02 us
    ppermute x1, starting transfers between devices, row_shards(): other = lax.ppermute(w_start, 'freq', swap)  3.03 us
    all_to_all x1, starting transfers between devices, exchange(): lax.all_to_all(value.astype(f16), axes, split_axis=0, concat_axis=0, tile...  2.58 us
    ppermute x1, starting transfers between devices, row_shards(): partner = lax.ppermute(acts, 'freq', swap)  1.72 us
  transfers between devices with their start and end apart: 6, of which 4 were waited for; matrix products, arithmetic and copies ran while one was open for 0% of the time, Pallas kernels for 11%

profile of v7, /device:TPU:0, one launch (start us, length us, event | category | flops | bytes accessed | tf_op | source)
XLA Modules:
  0.0 67.5 jit_solution(9638780782302075823)
XLA Ops:
  0.6 0.0 copy-start
  0.6 0.0 copy-start.1
  0.7 3.0 %collective-permute-start = (f32[32,2048]{1,0:T(8,128)}, f32[32,2048]{1,0:T(8,128)S(1)}, u32[]{:S(2)}, u32[]{:S(2)}) collective-permute-start(f32[32,2048]{1,0:T(8,128)} %own.1), channel_id=1, source_target_pairs={{0,16},{16,0},{1,17},{17,1},{2,18},{18,2},{3,19},{19,3},{4,20},{20... | collective-permute-start | bytes 786440 | tf_op jit(solution)/shard_map/ppermute | solution.py:501
  3.7 6.1 %spectrum.1 = (bf16[16,128,128]{2,1,0:T(8,128)(2,1)S(1)}, bf16[16,128,128]{2,1,0:T(8,128)(2,1)S(1)}, bf16[16,128]{1,0:T(8,128)(2,1)S(1)}) custom-call(s32[1]{0:T(128)} %bitcast.1.core, bf16[1,1048576]{1,0:T(2,128)(2,1)} %audio.1, f32[1216,128]{1,0:T(8,128)} %constant.24.clone.source), custom_call_target="tpu_custom_call" | custom-call | flops 2013265920 | bytes 4194304 | tf_op jit(solution)/shard_map/spectrum/pallas_call | solution.py:151
  9.8 0.1 collective-permute-start.2
  9.9 0.1 pad_add_fusion.at
  10.0 0.0 copy-done
  10.0 0.2 collective-permute-done.other
  10.2 0.0 copy-done.1
  10.2 1.4 %start.1 = (f32[32,128]{1,0:T(8,128)S(1)}, f32[32,128]{1,0:T(8,128)S(1)}) custom-call(s32[3]{0:T(128)S(1)} %pad_add_fusion.at, f32[32,2048]{1,0:T(8,128)S(1)} %copy-done.1, f32[32,2048]{1,0:T(8,128)S(1)} %collective-permute-done.other, bf16[16,128,128]{2,1,0:T(8,128)(2,1)S(1)} %get-tuple-element.16.keep, bf16[16,128,128]{2,1,0:T(8,128)(2,1)S(1)} %get-tuple-element.17.give, ...), custom_call_target="tpu_custom_call" | custom-call | flops 17179869184 | bytes 33554432 | tf_op jit(solution)/shard_map/start/pallas_call | solution.py:482
  11.6 0.4 collective-permute-start.1
  12.0 0.9 %collective-permute-done.1.sibling = f32[32,128]{1,0:T(8,128)S(1)} collective-permute-done((f32[32,128]{1,0:T(8,128)S(1)}, f32[32,128]{1,0:T(8,128)S(1)}, u32[]{:S(2)}, u32[]{:S(2)}) %collective-permute-start.1) | collective-permute-done | bytes 16416 | tf_op jit(solution)/shard_map/ppermute | solution.py:527
  12.9 0.0 collective-permute-done.2.taken
  12.9 0.5 sums.1
  13.4 15.1 %all_to_all.20 = f16[16,40,128]{2,1,0:T(8,128)(2,1)S(1)} all-to-all(f16[16,40,128]{2,1,0:T(8,128)(2,1)S(1)} %convert_element_type.29), channel_id=1, replica_groups=mesh['freq'=2,'chips'=8,'core'=2] {'freq','chips'}, dimensions={0} | all-to-all | bytes 327680 | tf_op jit(solution)/shard_map/all_to_all | solution.py:511
  28.5 0.5 slice.1
  29.0 11.0 %all_to_all.21 = f16[16,32,128]{2,1,0:T(8,128)(2,1)S(1)} all-to-all(f16[16,32,128]{2,1,0:T(8,128)(2,1)S(1)} %broadcast_in_dim.4), channel_id=1, replica_groups=mesh['freq'=2,'chips'=8,'core'=2] {'freq','chips'}, dimensions={0} | all-to-all | bytes 262144 | tf_op jit(solution)/shard_map/all_to_all | solution.py:511
  40.0 0.7 %partial.1.half = f32[72,128]{1,0:T(8,128)S(1)} custom-call(f32[16,32,128]{2,1,0:T(8,128)S(1)} %convert_element_type.32.got, f32[32,128]{1,0:T(8,128)S(1)} %get-tuple-element.21.exps, bf16[16,128,128]{2,1,0:T(8,128)(2,1)S(1)} %get-tuple-element.16.keep, bf16[16,128,128]{2,1,0:T(8,128)(2,1)S(1)} %collective-permute-done.2.taken, ...), custom_call_target="tpu_custom_call" | custom-call | tf_op jit(solution)/shard_map/partial/pallas_call | solution.py:482
  40.7 0.0 collective-permute-start.3
  40.8 1.2 %collective-permute-done.3.other_half = f32[72,128]{1,0:T(8,128)S(1)} collective-permute-done((f32[72,128]{1,0:T(8,128)S(1)}, f32[72,128]{1,0:T(8,128)S(1)}, u32[]{:S(2)}, u32[]{:S(2)}) %collective-permute-start.3) | collective-permute-done | bytes 36896 | tf_op jit(solution)/shard_map/ppermute | solution.py:534
  42.0 0.6 again.1
  42.6 11.0 %all_to_all.22 = f16[16,40,128]{2,1,0:T(8,128)(2,1)S(1)} all-to-all(f16[16,40,128]{2,1,0:T(8,128)(2,1)S(1)} %convert_element_type.33), channel_id=1, replica_groups=mesh['freq'=2,'chips'=8,'core'=2] {'freq','chips'}, dimensions={0} | all-to-all | bytes 327680 | tf_op jit(solution)/shard_map/all_to_all | solution.py:511
  53.7 0.7 last.1
  54.4 0.7 %broadcast_in_dim.10 = f16[2,16,16,128]{3,2,1,0:T(8,128)(2,1)} broadcast(f16[2,16,128]{2,1,0:T(8,128)(2,1)S(1)} %convert_element_type.35), dimensions={0,2,3} | broadcast | bytes 139264 | tf_op jit(solution)/shard_map/broadcast_in_dim | solution.py:543
  55.1 2.6 %all-to-all-start.3 = ((f16[32,16,128]{2,1,0:T(8,128)(2,1)}), f16[32,16,128]{2,1,0:T(8,128)(2,1)S(1)}, u32[]{:S(2)}, u32[]{:S(2)}) async-start(f16[32,16,128]{2,1,0:T(8,128)(2,1)} %bitcast.3), calls=%async_computation.3 | async-start | bytes 262144 | tf_op jit(solution)/shard_map/all_to_all | solution.py:511
  57.7 1.7 %collective-permute-start.4 = (f32[32,128]{1,0:T(8,128)S(1)}, f32[32,128]{1,0:T(8,128)S(1)}, u32[]{:S(2)}, u32[]{:S(2)}) collective-permute-start(f32[32,128]{1,0:T(8,128)S(1)} %get-tuple-element.29.acts), channel_id=1, source_target_pairs={{0,16},{16,0},{1,17},{17,1},{2,18},{18,2},{3,19},{19,3},{4,20},{20... | collective-permute-start | bytes 49160 | tf_op jit(solution)/shard_map/ppermute | solution.py:541
  59.4 6.5 %all-to-all-done.3 = f16[32,16,128]{2,1,0:T(8,128)(2,1)S(1)} async-done(((f16[32,16,128]{2,1,0:T(8,128)(2,1)}), f16[32,16,128]{2,1,0:T(8,128)(2,1)S(1)}, u32[]{:S(2)}, u32[]{:S(2)}) %all-to-all-start.3) | async-done | bytes 131104 | tf_op jit(solution)/shard_map/all_to_all | solution.py:511
  65.9 0.0 collective-permute-done.4.partner
  65.9 1.6 %natural.1 = (f32[32,2048]{1,0:T(8,128)}, f32[32,256]{1,0:T(8,128)}) custom-call(s32[3]{0:T(128)S(1)} %pad_add_fusion.at, f32[32,16,128]{2,1,0:T(8,128)S(1)} %convert_element_type.37.got, f32[32,128]{1,0:T(8,128)S(1)} %get-tuple-element.28.exps, f32[32,128]{1,0:T(8,128)S(1)} %get-tuple-element.29.acts, f32[32,128]{1,0:T(8,128)S(1)} %collective-permute-done.4.partner), custom_call_target="tpu_custom_call" | custom-call | tf_op jit(solution)/shard_map/natural/pallas_call | solution.py:482
  (10 shorter events, 0.2 us)
Async XLA Ops:
  0.6 9.4 %copy-start = (f32[32,256]{1,0:T(8,128)S(1)}, f32[32,256]{1,0:T(8,128)}, u32[]{:S(2)}) copy-start(f32[32,256]{1,0:T(8,128)} %param.6) | copy-start | bytes 98308
  0.6 9.6 %copy-start.1 = (f32[32,2048]{1,0:T(8,128)S(1)}, f32[32,2048]{1,0:T(8,128)}, u32[]{:S(2)}) copy-start(f32[32,2048]{1,0:T(8,128)} %own.1) | copy-start | bytes 786436
  0.7 9.5 %collective-permute-start = (f32[32,2048]{1,0:T(8,128)}, f32[32,2048]{1,0:T(8,128)S(1)}, u32[]{:S(2)}, u32[]{:S(2)}) collective-permute-start(f32[32,2048]{1,0:T(8,128)} %own.1), channel_id=1, source_target_pairs={{0,16},{16,0},{1,17},{17,1},{2,18},{18,2},{3,19},{19,3},{4,20},{20... | collective-permute-start | bytes 786440 | tf_op jit(solution)/shard_map/ppermute | solution.py:501
  9.8 3.0 %collective-permute-start.2 = (bf16[16,128,128]{2,1,0:T(8,128)(2,1)S(1)}, bf16[16,128,128]{2,1,0:T(8,128)(2,1)S(1)}, u32[]{:S(2)}, u32[]{:S(2)}) collective-permute-start(bf16[16,128,128]{2,1,0:T(8,128)(2,1)S(1)} %get-tuple-element.17.give), channel_id=1, source_target_pairs={{0,1},{1,0},{2,3},{3,2},{4,5},{5,4},{6,7},{7,6},{8,9},{9,8},{10,11... | collective-permute-start | bytes 1572872 | tf_op jit(solution)/shard_map/ppermute | solution.py:505
  11.6 1.2 %collective-permute-start.1 = (f32[32,128]{1,0:T(8,128)S(1)}, f32[32,128]{1,0:T(8,128)S(1)}, u32[]{:S(2)}, u32[]{:S(2)}) collective-permute-start(f32[32,128]{1,0:T(8,128)S(1)} %get-tuple-element.18.acts), channel_id=1, source_target_pairs={{0,1},{1,0},{2,3},{3,2},{4,5},{5,4},{6,7},{7,6},{8,9},{9,8},{10,11... | collective-permute-start | bytes 49160 | tf_op jit(solution)/shard_map/ppermute | solution.py:527
  40.7 1.2 %collective-permute-start.3 = (f32[72,128]{1,0:T(8,128)S(1)}, f32[72,128]{1,0:T(8,128)S(1)}, u32[]{:S(2)}, u32[]{:S(2)}) collective-permute-start(f32[72,128]{1,0:T(8,128)S(1)} %partial.1.half), channel_id=1, source_target_pairs={{0,1},{1,0},{2,3},{3,2},{4,5},{5,4},{6,7},{7,6},{8,9},{9,8},{10,11... | collective-permute-start | bytes 110600 | tf_op jit(solution)/shard_map/ppermute | solution.py:534
  55.1 10.8 %all-to-all-start.3 = ((f16[32,16,128]{2,1,0:T(8,128)(2,1)}), f16[32,16,128]{2,1,0:T(8,128)(2,1)S(1)}, u32[]{:S(2)}, u32[]{:S(2)}) async-start(f16[32,16,128]{2,1,0:T(8,128)(2,1)} %bitcast.3), calls=%async_computation.3 | async-start | bytes 262144 | tf_op jit(solution)/shard_map/all_to_all | solution.py:511
  57.7 8.3 %collective-permute-start.4 = (f32[32,128]{1,0:T(8,128)S(1)}, f32[32,128]{1,0:T(8,128)S(1)}, u32[]{:S(2)}, u32[]{:S(2)}) collective-permute-start(f32[32,128]{1,0:T(8,128)S(1)} %get-tuple-element.29.acts), channel_id=1, source_target_pairs={{0,16},{16,0},{1,17},{17,1},{2,18},{18,2},{3,19},{19,3},{4,20},{20... | collective-permute-start | bytes 49160 | tf_op jit(solution)/shard_map/ppermute | solution.py:541
